TPU v7x, 32 devices: a whole 2x2x4 slice. The times are simulated.
32 devices in a mesh: leaf: 32 (over z, y, x, core).
Axes of the slice: x: 2, y: 2, z: 4, core: 2. Of those that a mesh axis runs over, the one named last changes fastest.
Arguments:
- points: bfloat16 [64, 131072], P(None, 'leaf'), may hold values from -5 to 5
- charges: bfloat16 [32, 131072], P(None, 'leaf'), may hold values from -1.5 to 1.5
- leaf_order: int32 [32, 4096], P('leaf'), may hold values from 0 to 4095, each once within a row
- near_list: int32 [512, 16], P('leaf'), may hold values from -1 to 511, as said below
- far_list: int32 [256, 8], P('leaf'), may hold values from -1 to 7
- local_skel: int32 [480, 256], P('leaf'), may hold values from 0 to 511, as said below
- upper_skel: int32 [30, 256], replicated, may hold values from 0 to 511, as said below
Outputs:
- potentials: float32 [32, 131072], P(None, 'leaf')
- root_field: float32 [32, 32, 256], P('leaf')
Inputs may be any that keep to these rules, and one draw needn't show every extreme that they name: `leaf_order`: each row is a permutation of the positions of one device's points. `near_list`: slot 0 of leaf g's row is g itself; every other entry is -1 or a leaf h different from g with |h - g| <= 16, and the leaves of one row are distinct. `far_list`: an entry other than -1 names a level-one node of the same device subtree, counted from that subtree's first level-one node; entries of a row may repeat. `local_skel`: the entries of a row are distinct. `upper_skel`: the entries of a row are distinct.
All inputs are finite; a program needn't handle non-finite values.
Results may differ from a plain program's by a relative error of at most 0.0014.
Values may be sent and summed in bfloat16 or wider, within the bound.
No kernel may reach another device: no remote copies, remote signals or barrier semaphores. Data moves between devices by JAX's collectives and lax.ppermute only.
A program may use at most 64 MiB of HBM per device.

v0:
```python
import functools
import math

import jax
import jax.numpy as jnp
from jax import lax
from jax.experimental import pallas as pl
from jax.experimental.pallas import tpu as pltpu
from jax.sharding import PartitionSpec as P

PAIR_GAIN = math.sqrt(2.0)
LOG2E = math.log2(math.e)
BF = jnp.bfloat16
F32 = jnp.float32
NT = (((1,), (1,)), ((), ()))
AUX = 8
DEPTH = 128
BATCH = 8
VMEM = pl.BlockSpec(memory_space=pltpu.VMEM)
SMEM = pl.BlockSpec(memory_space=pltpu.SMEM)


def nt_dot(a, b):
    return lax.dot_general(a, b, NT, preferred_element_type=F32)


def nn_dot(a, b):
    return jnp.dot(a, b, preferred_element_type=F32)


def call(body, out_shape, in_specs, scratch, flops, limit_mb=24):
    return pl.pallas_call(
        body,
        out_shape=out_shape,
        in_specs=in_specs,
        out_specs=jax.tree.map(lambda _: VMEM, out_shape),
        scratch_shapes=scratch,
        compiler_params=pltpu.CompilerParams(vmem_limit_bytes=limit_mb * 2**20),
        cost_estimate=pl.CostEstimate(flops=flops, bytes_accessed=2**20, transcendentals=0),
    )


def kernel_tile(sq_dist, kern_scale):
    floor = jnp.maximum(sq_dist, 1e-30)
    root = floor * lax.rsqrt(floor)
    decay = jnp.exp2(root * (-kern_scale * LOG2E))
    return ((1.0 + root * kern_scale) * decay).astype(BF)


def aux_rows(x):
    width = x.shape[1]
    norm = jnp.sum(x * x, axis=0, keepdims=True)
    high = norm.astype(BF).astype(F32)
    rest = norm - high
    mid = rest.astype(BF).astype(F32)
    low = rest - mid
    row = lax.broadcasted_iota(jnp.int32, (AUX, width), 0)
    norms = jnp.where(row == 0, high, jnp.where(row == 1, mid, jnp.where(row == 2, low, 0.0)))
    ones = jnp.where(row < 3, 1.0, 0.0)
    return norms, ones


def source_form(x, norms, ones):
    pad = jnp.zeros((DEPTH - x.shape[0] - 2 * AUX, x.shape[1]), F32)
    return jnp.concatenate([x, norms, ones, pad], axis=0).astype(BF)


def target_form(x, norms, ones):
    pad = jnp.zeros((DEPTH - x.shape[0] - 2 * AUX, x.shape[1]), F32)
    return jnp.concatenate([-2.0 * x, ones, norms, pad], axis=0).T.astype(BF)


def split_form(selected, features):
    return (
        selected[:features],
        selected[features : features + AUX],
        selected[features + AUX : features + 2 * AUX],
    )


def one_hot(chosen, height):
    width = chosen.shape[1]
    row = lax.broadcasted_iota(jnp.int32, (height, width), 0)
    return jnp.where(row == chosen, 1.0, 0.0).astype(BF)


def gather_kernel(points, charges, order, stacked, grid, hots):
    features, total = points.shape
    rows = stacked.shape[0]
    width = hots.shape[1]
    blocks = total // width
    for b in range(blocks):
        cols = pl.ds(b * width, width)
        grid[b, :features] = points[:, cols]
        grid[b, features:] = charges[:, cols]
    for b in range(blocks):
        hots[b] = one_hot(order[:, pl.ds(b * width, width)] & (width - 1), width)

    def block(j, carry):
        start = pl.multiple_of(j * width, width)
        home = order[:, pl.ds(start, width)] // width
        spread = nn_dot(grid[...].reshape(blocks * rows, width), hots[j])
        total_rows = jnp.zeros((rows, width), F32)
        for b in range(blocks):
            mask = jnp.where(home == b, 1.0, 0.0)
            total_rows = total_rows + spread[b * rows : (b + 1) * rows] * mask
        stacked[:, pl.ds(start, width)] = total_rows.astype(BF)
        return carry

    lax.fori_loop(0, blocks, block, 0)


def lift(sources, weights, target, kern_scale):
    kernel = kernel_tile(nn_dot(target, sources), kern_scale)
    sums = nt_dot(weights, kernel)
    rhs = weights.shape[0] - 16
    lifted = PAIR_GAIN * (sums[:rhs] / sums[rhs : rhs + 1])
    return kernel, lifted


def with_ones(weights):
    return jnp.concatenate([weights, jnp.ones((16, weights.shape[1]), weights.dtype)], axis=0)


def tree_kernel(
    kern_scale, features, stacked, skel,
    leaf_src, leaf_tgt, leaf_wts, src1, tgt1, wts1, src_up, tgt_up, wts_up, kernels, payload,
    joined, joined_w,
):
    leaves = leaf_src.shape[0]
    width = leaf_src.shape[2]
    for leaf in range(leaves):
        cols = pl.ds(leaf * width, width)
        x = stacked[:features, cols].astype(F32)
        norms, ones = aux_rows(x)
        leaf_src[leaf] = source_form(x, norms, ones)
        leaf_tgt[leaf] = target_form(x, norms, ones)
        leaf_wts[leaf] = stacked[features:, cols]
    depth = leaves.bit_length() - 1
    live = features + 2 * AUX
    row = 0
    for height in range(1, depth + 1):
        for node in range(leaves >> height):
            if height == 1:
                src, wts, first = leaf_src, leaf_wts, 2 * node
            elif height == 2:
                src, wts, first = src1, wts1, 2 * node
            else:
                below = (leaves // 2) - (leaves >> (height - 2))
                src, wts, first = src_up, wts_up, below + 2 * node
            slot = row % 8
            for half in range(2):
                joined[slot, :, half * width : (half + 1) * width] = src[first + half]
                joined_w[slot, :, half * width : (half + 1) * width] = with_ones(wts[first + half])
            hot = one_hot(skel[row : row + 1, :], 2 * width)
            x, norms, ones = split_form(nn_dot(joined[slot, :live], hot), features)
            own_src = source_form(x, norms, ones)
            own_tgt = target_form(x, norms, ones)
            kernel, lifted = lift(joined[slot], joined_w[slot], own_tgt, kern_scale)
            kernels[row] = kernel
            own_wts = lifted.astype(BF)
            if height == 1:
                src1[node], tgt1[node], wts1[node] = own_src, own_tgt, own_wts
            else:
                at = row - leaves // 2
                src_up[at], tgt_up[at], wts_up[at] = own_src, own_tgt, own_wts
            if height == depth:
                payload[:live] = own_src[:live]
                payload[live:] = own_wts
            row += 1


def padded(rows):
    return jnp.concatenate(
        [rows, jnp.zeros((DEPTH - rows.shape[0], rows.shape[1]), rows.dtype)], axis=0
    )


def couple_kernel(kern_scale, live, sibling, own_tgt, field):
    kernel = kernel_tile(nn_dot(own_tgt[...], padded(sibling[:live])), kern_scale)
    field[...] = nt_dot(sibling[live:], kernel)


def chain_kernel(
    kern_scale, features, place, own, sibling, own_tgt, skel,
    field, next_own, next_tgt, half_kernel, joined, joined_w,
):
    live = features + 2 * AUX
    width = own.shape[1]
    kernel = kernel_tile(nn_dot(own_tgt[...], padded(sibling[:live])), kern_scale)
    field[...] = nt_dot(sibling[live:], kernel)
    joined[:, :width] = padded(own[:live])
    joined[:, width:] = padded(sibling[:live])
    joined_w[:, :width] = with_ones(own[live:])
    joined_w[:, width:] = with_ones(sibling[live:])
    chosen = skel[pl.ds(place[0], 1), :]
    chosen = chosen + place[1] * jnp.where(chosen < width, width, -width)
    hot = one_hot(chosen, 2 * width)
    x, norms, ones = split_form(nn_dot(joined[:live], hot), features)
    target = target_form(x, norms, ones)
    kernel, lifted = lift(joined[...], joined_w[...], target, kern_scale)
    half_kernel[...] = kernel[:, :width]
    next_tgt[...] = target
    next_own[:live] = source_form(x, norms, ones)[:live]
    next_own[live:] = lifted.astype(BF)


def pair_loop(kern_scale, pairs, count, src, tgt, wts, acc):
    last = tgt.shape[0] - 1

    def batch(i, carry):
        terms = []
        for u in range(BATCH):
            code = pairs[i * BATCH + u]
            h = code & 255
            g = code >> 8
            kernel = kernel_tile(nn_dot(tgt[jnp.minimum(g, last)], src[h]), kern_scale)
            terms.append((g, nt_dot(wts[h], kernel)))
        for g, term in terms:
            acc[g] = acc[g] + term
        return carry

    lax.fori_loop(0, (count + (BATCH - 1)) >> 3, batch, 0)


def finish_list(pairs, count, dummy):
    for u in range(BATCH):
        pairs[count + u] = dummy << 8


def near_own_kernel(kern_scale, first, near, place, src, tgt, wts, out, pairs, acc):
    targets = out.shape[0]
    leaves = src.shape[0]
    slots = near.shape[1]
    base = place[0] * leaves
    acc[...] = jnp.zeros_like(acc)
    count = jnp.int32(0)
    for t in range(targets):
        for s in range(slots):
            h = near[first + t, s] - base
            pairs[count] = h + ((first + t) << 8)
            count = count + jnp.where((h >= 0) & (h < leaves), 1, 0)
    finish_list(pairs, count, leaves)
    pair_loop(kern_scale, pairs, count, src, tgt, wts, acc)
    out[...] = acc[pl.ds(first, targets)]


def far_kernel(kern_scale, far, src, tgt, wts, out, pairs, counts, acc):
    nodes = src.shape[0]
    slots = far.shape[1]
    for i in range(nodes):
        for b in range(nodes):
            counts[i, b] = jnp.int32(1 if b == (i ^ 1) else 0)
        counts[i, nodes] = jnp.int32(0)
        for s in range(slots):
            e = far[i, s]
            at = jnp.where(e < 0, nodes, e)
            counts[i, at] = counts[i, at] + 1
    total = jnp.int32(0)
    for i in range(nodes):
        for b in range(nodes):
            pairs[total] = b + (i << 8)
            total = total + jnp.where(counts[i, b] > 0, 1, 0)
    finish_list(pairs, total, nodes)
    for b in range(nodes):
        counts[nodes, b] = jnp.int32(0)
    acc[...] = jnp.zeros_like(acc)
    last = nodes - 1

    def batch(i, carry):
        terms = []
        for u in range(BATCH):
            code = pairs[i * BATCH + u]
            h = code & 255
            g = code >> 8
            kernel = kernel_tile(nn_dot(tgt[jnp.minimum(g, last)], src[h]), kern_scale)
            times = counts[g, h].astype(F32)
            terms.append((g, nt_dot(wts[h], kernel) * times))
        for g, term in terms:
            acc[g] = acc[g] + term
        return carry

    lax.fori_loop(0, (total + (BATCH - 1)) >> 3, batch, 0)
    out[...] = acc[pl.ds(0, nodes)]


def down_kernel(
    kern_scale, upper, leaves, kernels, field1, src_up, tgt_up, wts_up, *rest
):
    chain_fields = rest[:upper]
    half_kernels = rest[upper : 2 * upper - 1]
    root, leaf_field = rest[2 * upper - 1 :]
    width = root.shape[1]
    depth = leaves.bit_length() - 1
    rhs = root.shape[0]

    def push(field, kernel):
        sums = nn_dot(with_ones(field.astype(BF)), kernel)
        return sums[:rhs] / sums[rhs : rhs + 1]

    field = chain_fields[upper - 1][...]
    for bit in range(upper - 2, -1, -1):
        field = chain_fields[bit][...] + push(field, half_kernels[bit][...])
    root[...] = field
    fields = [field]
    for height in range(depth, 0, -1):
        first_row = leaves - (leaves >> (height - 1))
        below = []
        for node in range(leaves >> height):
            pushed = push(fields[node], kernels[first_row + node])
            below += [pushed[:, :width], pushed[:, width:]]
        if height == 1:
            for leaf in range(leaves):
                leaf_field[leaf] = below[leaf]
        else:
            fields = []
            first = leaves // 2 - (leaves >> (height - 2))
            for node in range(leaves >> (height - 1)):
                if height == 2:
                    coupled = field1[node]
                else:
                    at = first + (node ^ 1)
                    kernel = kernel_tile(nn_dot(tgt_up[first + node], src_up[at]), kern_scale)
                    coupled = nt_dot(wts_up[at], kernel)
                fields.append(coupled + below[node])


def final_kernel(
    kern_scale, features, near, place, left, right, tgt, order, leaf_field, *rest
):
    *own_parts, out, src, wts, acc, pairs, spread = rest
    leaves, width, _ = tgt.shape
    slots = near.shape[1]
    rhs = out.shape[0]
    for side, halo in enumerate((left, right)):
        for leaf in range(leaves):
            cols = pl.ds(leaf * width, width)
            x = halo[:features, cols].astype(F32)
            src[side * leaves + leaf] = source_form(x, *aux_rows(x))
            wts[side * leaves + leaf] = halo[features:, cols]
    at = 0
    for part in own_parts:
        for t in range(part.shape[0]):
            acc[at] = part[t] + leaf_field[at]
            at += 1
    acc[leaves] = jnp.zeros_like(acc[leaves])
    base = place[0] * leaves

    def scan(g, count):
        for s in range(slots):
            entry = near[g, s]
            h = entry - base
            go_left = (entry >= 0) & (h < 0)
            go_right = h >= leaves
            at = jnp.where(go_right, h, h + leaves)
            pairs[count] = at + (g << 8)
            count = count + jnp.where(go_left | go_right, 1, 0)
        return count

    count = lax.fori_loop(0, leaves, scan, jnp.int32(0))
    finish_list(pairs, count, leaves)
    pair_loop(kern_scale, pairs, count, src, tgt, wts, acc)
    spread[...] = jnp.zeros_like(spread)

    def scatter(leaf, carry):
        start = pl.multiple_of(leaf * width, width)
        index = order[:, pl.ds(start, width)]
        home = index // width
        hot_t = one_hot(index & (width - 1), width)
        rows = acc[leaf]
        high = rows.astype(BF)
        low = (rows - high.astype(F32)).astype(BF)
        both = jnp.concatenate([high, low], axis=0)
        stack = []
        for b in range(leaves):
            mask = jnp.where(home == b, 1.0, 0.0).astype(BF)
            stack.append(both * mask)
        spread[...] += nt_dot(jnp.concatenate(stack, axis=0), hot_t)
        return carry

    lax.fori_loop(0, leaves, scatter, 0)
    for b in range(leaves):
        at = b * 2 * rhs
        out[:, pl.ds(b * width, width)] = spread[pl.ds(at, rhs)] + spread[pl.ds(at + rhs, rhs)]


def local(points, charges, leaf_order, near_list, far_list, local_skel, upper_skel):
    features, total = points.shape
    rhs = charges.shape[0]
    leaves, _ = near_list.shape
    width = local_skel.shape[1]
    nodes = local_skel.shape[0]
    kern_scale = 2.0 * math.sqrt(3.0 / features)
    devices = lax.axis_size("leaf")
    upper = devices.bit_length() - 1
    position = lax.axis_index("leaf")
    live = features + 2 * AUX
    rows = features + rhs
    shape = jax.ShapeDtypeStruct
    place = jnp.reshape(position, (1,)).astype(jnp.int32)

    stacked = call(
        gather_kernel,
        shape((rows, total), BF),
        [VMEM] * 3,
        [pltpu.VMEM((leaves, rows, width), BF), pltpu.VMEM((leaves, width, width), BF)],
        10**10,
    )(points, charges, leaf_order)
    ring = list(range(devices - 1))
    left = lax.ppermute(stacked, "leaf", [(i, i + 1) for i in ring])
    right = lax.ppermute(stacked, "leaf", [(i + 1, i) for i in ring])

    half, top = leaves // 2, nodes - leaves // 2
    (leaf_src, leaf_tgt, leaf_wts, src1, tgt1, wts1, src_up, tgt_up, wts_up, kernels, payload) = call(
        functools.partial(tree_kernel, kern_scale, features),
        (
            shape((leaves, DEPTH, width), BF),
            shape((leaves, width, DEPTH), BF),
            shape((leaves, rhs, width), BF),
            shape((half, DEPTH, width), BF),
            shape((half, width, DEPTH), BF),
            shape((half, rhs, width), BF),
            shape((top, DEPTH, width), BF),
            shape((top, width, DEPTH), BF),
            shape((top, rhs, width), BF),
            shape((nodes, width, 2 * width), BF),
            shape((live + rhs, width), BF),
        ),
        [VMEM] * 2,
        [pltpu.VMEM((8, DEPTH, 2 * width), BF), pltpu.VMEM((8, rhs + 16, 2 * width), BF)],
        10**10,
    )(stacked, local_skel)

    cuts = [leaves * k // (upper - 1) for k in range(upper)]
    own_parts = []
    for k in range(upper - 1):
        count = cuts[k + 1] - cuts[k]
        if count == 0:
            continue
        own_parts.append(
            call(
                functools.partial(near_own_kernel, kern_scale, cuts[k]),
                shape((count, rhs, width), F32),
                [SMEM] * 2 + [VMEM] * 3,
                [
                    pltpu.SMEM((count * near_list.shape[1] + BATCH,), jnp.int32),
                    pltpu.VMEM((leaves + 1, rhs, width), F32),
                ],
                2 * 10**9,
            )(near_list, place, leaf_src, leaf_tgt, leaf_wts)
        )
    field1 = call(
        functools.partial(far_kernel, kern_scale),
        shape((half, rhs, width), F32),
        [SMEM] + [VMEM] * 3,
        [
            pltpu.SMEM((half * half + BATCH,), jnp.int32),
            pltpu.SMEM((half + 1, half + 1), jnp.int32),
            pltpu.VMEM((half + 1, rhs, width), F32),
        ],
        4 * 10**9,
    )(far_list, src1, tgt1, wts1)

    own, own_tgt = payload, tgt_up[top - 1]
    chain_fields, half_kernels = [], []
    for bit in range(upper):
        sibling = lax.ppermute(own, "leaf", [(i, i ^ (1 << bit)) for i in range(devices)])
        if bit == upper - 1:
            chain_fields.append(
                call(
                    functools.partial(couple_kernel, kern_scale, live),
                    shape((rhs, width), F32),
                    [VMEM] * 2,
                    [],
                    10**8,
                )(sibling, own_tgt)
            )
            break
        table_row = devices - (devices >> bit) + (position >> (bit + 1))
        where = jnp.stack([table_row, (position >> bit) & 1]).astype(jnp.int32)
        field, own, own_tgt, half_kernel = call(
            functools.partial(chain_kernel, kern_scale, features),
            (
                shape((rhs, width), F32),
                shape((live + rhs, width), BF),
                shape((width, DEPTH), BF),
                shape((width, width), BF),
            ),
            [SMEM] + [VMEM] * 4,
            [pltpu.VMEM((DEPTH, 2 * width), BF), pltpu.VMEM((rhs + 16, 2 * width), BF)],
            10**8,
        )(where, own, sibling, own_tgt, upper_skel)
        chain_fields.append(field)
        half_kernels.append(half_kernel)

    root, leaf_field = call(
        functools.partial(down_kernel, kern_scale, upper, leaves),
        (shape((rhs, width), F32), shape((leaves, rhs, width), F32)),
        [VMEM] * (5 + 2 * upper - 1),
        [],
        10**9,
    )(kernels, field1, src_up, tgt_up, wts_up, *chain_fields, *half_kernels)

    potentials = call(
        functools.partial(final_kernel, kern_scale, features),
        shape((rhs, total), F32),
        [SMEM] * 2 + [VMEM] * (5 + len(own_parts)),
        [
            pltpu.VMEM((2 * leaves, DEPTH, width), BF),
            pltpu.VMEM((2 * leaves, rhs, width), BF),
            pltpu.VMEM((leaves + 1, rhs, width), F32),
            pltpu.SMEM((near_list.size + BATCH,), jnp.int32),
            pltpu.VMEM((leaves * 2 * rhs, width), F32),
        ],
        10**10,
    )(near_list, place, left, right, leaf_tgt, leaf_order, leaf_field, *own_parts)
    return (potentials, root[None])


def solution(mesh):
    placed = (
        P(None, "leaf"),
        P(None, "leaf"),
        P("leaf", None),
        P("leaf", None),
        P("leaf", None),
        P("leaf", None),
        P(),
    )
    return jax.shard_map(
        local,
        mesh=mesh,
        in_specs=placed,
        out_specs=(P(None, "leaf"), P("leaf", None, None)),
        check_vma=False,
    )
```

profile of v0, /device:TPU:8, one launch (start us, length us, event | category | flops | bytes accessed | tf_op | source)
XLA Modules:
  0.0 104.9 jit_solution(12694684173290370209)
XLA Ops:
  0.6 1.0 copy-done.2
  1.7 0.9 copy-done.3
  2.6 0.7 copy-done.6
  3.3 6.7 %shard_map.86.stacked = bf16[96,4096]{1,0:T(8,128)(2,1)S(1)} custom-call(bf16[64,4096]{1,0:T(8,128)(2,1)S(1)} %copy-done.2, bf16[32,4096]{1,0:T(8,128)(2,1)S(1)} %copy-done.3, s32[1,4096]{1,0:T(1,128)S(1)} %copy-done.6), custom_call_target="tpu_custom_call" | custom-call | flops 10000000000 | bytes 1048576 | tf_op jit(solution)/shard_map/pallas_call | solution.py:402
  10.1 1.9 %collective-permute-start = (bf16[96,4096]{1,0:T(8,128)(2,1)S(1)}, bf16[96,4096]{1,0:T(8,128)(2,1)S(1)}, u32[]{:S(2)}, u32[]{:S(2)}) collective-permute-start(bf16[96,4096]{1,0:T(8,128)(2,1)S(1)} %shard_map.86.stacked), channel_id=1, source_target_pairs={{0,1},{1,2},{2,3},{3,4},{4,5},{5,6},{6,7},{7,8},{8,9},{9,10},{10,1... | collective-permute-start | bytes 2359304 | tf_op jit(solution)/shard_map/ppermute | solution.py:410
  12.0 5.4 %collective-permute-start.1 = (bf16[96,4096]{1,0:T(8,128)(2,1)S(1)}, bf16[96,4096]{1,0:T(8,128)(2,1)}, u32[]{:S(2)}, u32[]{:S(2)}) collective-permute-start(bf16[96,4096]{1,0:T(8,128)(2,1)S(1)} %shard_map.86.stacked), channel_id=1, source_target_pairs={{1,0},{2,1},{3,2},{4,3},{5,4},{6,5},{7,6},{8,7},{9,8},{10,9},{11,1... | collective-permute-start | bytes 2359304 | tf_op jit(solution)/shard_map/ppermute | solution.py:411
  17.5 5.9 %shard_map.87 = (bf16[16,128,256]{2,1,0:T(8,128)(2,1)S(1)}, bf16[16,256,128]{2,1,0:T(8,128)(2,1)S(1)}, bf16[16,32,256]{2,1,0:T(8,128)(2,1)S(1)}, bf16[8,128,256]...) custom-call(bf16[96,4096]{1,0:T(8,128)(2,1)S(1)} %shard_map.86.stack, ...), custom_call_target="tpu_custom_call" | custom-call | flops 10000000000 | bytes 1048576 | tf_op jit(solution)/shard_map/pallas_call | solution.py:414
  23.4 1.9 %copy-done = bf16[15,256,512]{2,1,0:T(8,128)(2,1)} copy-done((bf16[15,256,512]{2,1,0:T(8,128)(2,1)}, bf16[15,256,512]{2,1,0:T(8,128)(2,1)S(1)}, u32[]{:S(2)}) %copy-start) | copy-done | bytes 3932184
  25.3 1.0 copy-done.10
  26.3 1.0 copy-done.15
  27.2 0.8 copy-done.23
  28.0 0.8 copy-done.25
  28.8 1.3 %copy-done.11 = bf16[16,256,128]{2,1,0:T(8,128)(2,1)S(1)} copy-done((bf16[16,256,128]{2,1,0:T(8,128)(2,1)S(1)}, bf16[16,256,128]{2,1,0:T(8,128)(2,1)}, u32[]{:S(2)}) %copy-start.11) | copy-done | bytes 1048600
  30.1 1.2 %copy-done.16 = bf16[16,128,256]{2,1,0:T(8,128)(2,1)S(1)} copy-done((bf16[16,128,256]{2,1,0:T(8,128)(2,1)S(1)}, bf16[16,128,256]{2,1,0:T(8,128)(2,1)}, u32[]{:S(2)}) %copy-start.16) | copy-done | bytes 1048600
  31.3 5.4 %shard_map.98.rest_3_ = f32[4,32,256]{2,1,0:T(8,128)S(1)} custom-call(s32[16,16]{1,0:T(8,128)S(1)} %copy-done.8, s32[1]{0:T(128)} %bitcast.place, bf16[16,128,256]{2,1,0:T(8,128)(2,1)S(1)} %copy-done.16, bf16[16,256,128]{2,1,0:T(8,128)(2,1)S(1)} %copy-done.11, bf16[16,32,256]{2,1,0:T(8,128)(2,1)S(1)} %get-tuple-element.58.wts), custom_call_target="tpu_custom_call" | custom-call | flops 2000000000 | bytes 1048576 | tf_op jit(solution)/shard_map/pallas_call | solution.py:441
  36.7 4.5 %shard_map.97.rest_2_ = f32[4,32,256]{2,1,0:T(8,128)S(1)} custom-call(s32[16,16]{1,0:T(8,128)S(1)} %copy-done.8, s32[1]{0:T(128)} %bitcast.place, bf16[16,128,256]{2,1,0:T(8,128)(2,1)S(1)} %copy-done.16, bf16[16,256,128]{2,1,0:T(8,128)(2,1)S(1)} %copy-done.11, bf16[16,32,256]{2,1,0:T(8,128)(2,1)S(1)} %get-tuple-element.58.wts), custom_call_target="tpu_custom_call" | custom-call | flops 2000000000 | bytes 1048576 | tf_op jit(solution)/shard_map/pallas_call | solution.py:441
  41.3 0.9 copy-done.28
  42.2 6.5 %shard_map.88.field1 = f32[8,32,256]{2,1,0:T(8,128)S(1)} custom-call(s32[8,8]{1,0:T(8,128)S(1)} %copy-done.9, bf16[8,128,256]{2,1,0:T(8,128)(2,1)S(1)} %copy-done.24, bf16[8,256,128]{2,1,0:T(8,128)(2,1)S(1)} %copy-done.26, bf16[8,32,256]{2,1,0:T(8,128)(2,1)S(1)} %copy-done.28), custom_call_target="tpu_custom_call" | custom-call | flops 4000000000 | bytes 1048576 | tf_op jit(solution)/shard_map/pallas_call | solution.py:452
  48.8 4.6 %shard_map.96.rest_1_ = f32[4,32,256]{2,1,0:T(8,128)S(1)} custom-call(s32[16,16]{1,0:T(8,128)S(1)} %copy-done.8, s32[1]{0:T(128)} %bitcast.place, bf16[16,128,256]{2,1,0:T(8,128)(2,1)S(1)} %copy-done.17, bf16[16,256,128]{2,1,0:T(8,128)(2,1)S(1)} %copy-done.12, bf16[16,32,256]{2,1,0:T(8,128)(2,1)S(1)} %get-tuple-element.58.wts), custom_call_target="tpu_custom_call" | custom-call | flops 2000000000 | bytes 1048576 | tf_op jit(solution)/shard_map/pallas_call | solution.py:441
  54.1 1.3 %shard_map.89 = (f32[32,256]{1,0:T(8,128)S(1)}, bf16[112,256]{1,0:T(8,128)(2,1)S(1)}, bf16[256,128]{1,0:T(8,128)(2,1)S(1)}, bf16[256,256]{1,0:T(8,128)(2,1)S(1)}) custom-call(s32[2]{0:T(128)S(1)} %pad_add_fusion.place, bf16[112,256]{1,0:T(8,128)(2,1)S(1)} %get-tuple-element.39.own, bf16[112,256]{1,0:T(8,128)(2,1)S(1)} %collective-permute-done.2.sibling, ...), custom_call_target="tpu_custom_call" | custom-call | flops 100000000 | bytes 1048576 | tf_op jit(solution)/shard_map/pallas_call | solution.py:481
  55.5 4.1 %collective-permute-done.3.sibling = bf16[112,256]{1,0:T(8,128)(2,1)S(1)} collective-permute-done((bf16[112,256]{1,0:T(8,128)(2,1)S(1)}, bf16[112,256]{1,0:T(8,128)(2,1)S(1)}, u32[]{:S(2)}, u32[]{:S(2)}) %collective-permute-start.3) | collective-permute-done | bytes 57376 | tf_op jit(solution)/shard_map/ppermute | solution.py:467
  59.6 1.3 %shard_map.90 = (f32[32,256]{1,0:T(8,128)S(1)}, bf16[112,256]{1,0:T(8,128)(2,1)S(1)}, bf16[256,128]{1,0:T(8,128)(2,1)S(1)}, bf16[256,256]{1,0:T(8,128)(2,1)S(1)}) custom-call(s32[2]{0:T(128)S(1)} %pad_add_fusion.1.place, bf16[112,256]{1,0:T(8,128)(2,1)S(1)} %get-tuple-element.41.own, bf16[112,256]{1,0:T(8,128)(2,1)S(1)} %collective-permute-done.3.sibling, ...), custom_call_target="tpu_custom_call" | custom-call | flops 100000000 | bytes 1048576 | tf_op jit(solution)/shard_map/pallas_call | solution.py:481
  61.0 4.1 %collective-permute-done.4.sibling = bf16[112,256]{1,0:T(8,128)(2,1)S(1)} collective-permute-done((bf16[112,256]{1,0:T(8,128)(2,1)S(1)}, bf16[112,256]{1,0:T(8,128)(2,1)S(1)}, u32[]{:S(2)}, u32[]{:S(2)}) %collective-permute-start.4) | collective-permute-done | bytes 57376 | tf_op jit(solution)/shard_map/ppermute | solution.py:467
  65.1 1.3 %shard_map.91 = (f32[32,256]{1,0:T(8,128)S(1)}, bf16[112,256]{1,0:T(8,128)(2,1)S(1)}, bf16[256,128]{1,0:T(8,128)(2,1)S(1)}, bf16[256,256]{1,0:T(8,128)(2,1)S(1)}) custom-call(s32[2]{0:T(128)S(1)} %pad_add_fusion.2.place, bf16[112,256]{1,0:T(8,128)(2,1)S(1)} %get-tuple-element.44.own, bf16[112,256]{1,0:T(8,128)(2,1)S(1)} %collective-permute-done.4.sibling, ...), custom_call_target="tpu_custom_call" | custom-call | flops 100000000 | bytes 1048576 | tf_op jit(solution)/shard_map/pallas_call | solution.py:481
  66.5 4.1 %collective-permute-done.5.sibling = bf16[112,256]{1,0:T(8,128)(2,1)S(1)} collective-permute-done((bf16[112,256]{1,0:T(8,128)(2,1)S(1)}, bf16[112,256]{1,0:T(8,128)(2,1)S(1)}, u32[]{:S(2)}, u32[]{:S(2)}) %collective-permute-start.5) | collective-permute-done | bytes 57376 | tf_op jit(solution)/shard_map/ppermute | solution.py:467
  70.6 1.3 %shard_map.92 = (f32[32,256]{1,0:T(8,128)S(1)}, bf16[112,256]{1,0:T(8,128)(2,1)S(1)}, bf16[256,128]{1,0:T(8,128)(2,1)S(1)}, bf16[256,256]{1,0:T(8,128)(2,1)S(1)}) custom-call(s32[2]{0:T(128)S(1)} %pad_add_fusion.3.place, bf16[112,256]{1,0:T(8,128)(2,1)S(1)} %get-tuple-element.47.own, bf16[112,256]{1,0:T(8,128)(2,1)S(1)} %collective-permute-done.5.sibling, ...), custom_call_target="tpu_custom_call" | custom-call | flops 100000000 | bytes 1048576 | tf_op jit(solution)/shard_map/pallas_call | solution.py:481
  71.9 2.7 %collective-permute-start.6 = (bf16[112,256]{1,0:T(8,128)(2,1)S(1)}, bf16[112,256]{1,0:T(8,128)(2,1)S(1)}, u32[]{:S(2)}, u32[]{:S(2)}) collective-permute-start(bf16[112,256]{1,0:T(8,128)(2,1)S(1)} %get-tuple-element.50), channel_id=1, source_target_pairs={{0,16},{1,17},{2,18},{3,19},{4,20},{5,21},{6,22},{7,23},{8,24},{9,... | collective-permute-start | bytes 172040 | tf_op jit(solution)/shard_map/ppermute | solution.py:467
  74.6 1.2 %copy-done.13 = bf16[16,256,128]{2,1,0:T(8,128)(2,1)S(1)} copy-done((bf16[16,256,128]{2,1,0:T(8,128)(2,1)S(1)}, bf16[16,256,128]{2,1,0:T(8,128)(2,1)}, u32[]{:S(2)}) %copy-start.13) | copy-done | bytes 1048600
  75.8 1.2 %copy-done.18 = bf16[16,128,256]{2,1,0:T(8,128)(2,1)S(1)} copy-done((bf16[16,128,256]{2,1,0:T(8,128)(2,1)S(1)}, bf16[16,128,256]{2,1,0:T(8,128)(2,1)}, u32[]{:S(2)}) %copy-start.18) | copy-done | bytes 1048600
  77.0 4.5 %shard_map.95.rest_0_ = f32[4,32,256]{2,1,0:T(8,128)S(1)} custom-call(s32[16,16]{1,0:T(8,128)S(1)} %copy-done.8, s32[1]{0:T(128)} %bitcast.place, bf16[16,128,256]{2,1,0:T(8,128)(2,1)S(1)} %copy-done.18, bf16[16,256,128]{2,1,0:T(8,128)(2,1)S(1)} %copy-done.13, bf16[16,32,256]{2,1,0:T(8,128)(2,1)S(1)} %get-tuple-element.58.wts), custom_call_target="tpu_custom_call" | custom-call | flops 2000000000 | bytes 1048576 | tf_op jit(solution)/shard_map/pallas_call | solution.py:441
  81.9 2.3 %shard_map.94 = (f32[32,256]{1,0:T(8,128)}, f32[16,32,256]{2,1,0:T(8,128)S(1)}) custom-call(bf16[15,256,512]{2,1,0:T(8,128)(2,1)S(1)} %copy-done.1, f32[8,32,256]{2,1,0:T(8,128)S(1)} %shard_map.88.field1, bf16[7,128,256]{2,1,0:T(8,128)(2,1)S(1)} %get-tuple-element.36.src_up, bf16[7,256,128]{2,1,0:T(8,128)(2,1)S(1)} %get-tuple-element.37.tgt_up, ...), custom_call_target="tpu_custom_call" | custom-call | flops 1000000000 | bytes 1048576 | tf_op jit(solution)/shard_map/pallas_call | solution.py:496
  84.3 20.6 %shard_map.99 = f32[32,4096]{1,0:T(8,128)} custom-call(s32[16,16]{1,0:T(8,128)S(1)} %copy-done.8, s32[1]{0:T(128)} %bitcast.place, bf16[96,4096]{1,0:T(8,128)(2,1)S(1)} %collective-permute-done.left, bf16[96,4096]{1,0:T(8,128)(2,1)} %collective-permute-done.1.right, bf16[16,256,128]{2,1,0:T(8,128)(2,1)S(1)} %copy-done.14, s32[1,4096]{1,0:T(1,128)S(1)} %copy-done.7, ...), custom_call_target="tpu_custom_call" | custom-call | flops 10000000000 | bytes 1048576 | tf_op jit(solution)/shard_map/pallas_call | solution.py:504
  (59 shorter events, 1.6 us)
Async XLA Ops:
  0.6 1.0 copy-start.2
  1.7 0.9 copy-start.3
  3.3 14.1 %copy-start.5 = (s32[15,256]{1,0:T(8,128)S(1)}, s32[15,256]{1,0:T(8,128)}, u32[]{:S(2)}) copy-start(s32[15,256]{1,0:T(8,128)} %skel.5) | copy-start | bytes 46084
  10.1 18.8 %copy-start.8 = (s32[16,16]{1,0:T(8,128)S(1)}, s32[16,16]{1,0:T(8,128)}, u32[]{:S(2)}) copy-start(s32[16,16]{1,0:T(8,128)} %near.9) | copy-start | bytes 3076
  10.1 74.1 %collective-permute-start = (bf16[96,4096]{1,0:T(8,128)(2,1)S(1)}, bf16[96,4096]{1,0:T(8,128)(2,1)S(1)}, u32[]{:S(2)}, u32[]{:S(2)}) collective-permute-start(bf16[96,4096]{1,0:T(8,128)(2,1)S(1)} %shard_map.86.stacked), channel_id=1, source_target_pairs={{0,1},{1,2},{2,3},{3,4},{4,5},{5,6},{6,7},{7,8},{8,9},{9,10},{10,1... | collective-permute-start | bytes 2359304 | tf_op jit(solution)/shard_map/ppermute | solution.py:410
  12.0 72.2 %collective-permute-start.1 = (bf16[96,4096]{1,0:T(8,128)(2,1)S(1)}, bf16[96,4096]{1,0:T(8,128)(2,1)}, u32[]{:S(2)}, u32[]{:S(2)}) collective-permute-start(bf16[96,4096]{1,0:T(8,128)(2,1)S(1)} %shard_map.86.stacked), channel_id=1, source_target_pairs={{1,0},{2,1},{3,2},{4,3},{5,4},{6,5},{7,6},{8,7},{9,8},{10,9},{11,1... | collective-permute-start | bytes 2359304 | tf_op jit(solution)/shard_map/ppermute | solution.py:411
  23.4 1.9 %copy-start = (bf16[15,256,512]{2,1,0:T(8,128)(2,1)}, bf16[15,256,512]{2,1,0:T(8,128)(2,1)S(1)}, u32[]{:S(2)}) copy-start(bf16[15,256,512]{2,1,0:T(8,128)(2,1)S(1)} %get-tuple-element.32.kernels) | copy-start | bytes 11796484
  25.2 1.0 copy-start.10
  26.3 1.0 copy-start.15
  28.8 12.4 %copy-start.27 = (bf16[8,32,256]{2,1,0:T(8,128)(2,1)}, bf16[8,32,256]{2,1,0:T(8,128)(2,1)S(1)}, u32[]{:S(2)}) copy-start(bf16[8,32,256]{2,1,0:T(8,128)(2,1)S(1)} %get-tuple-element.35.wts) | copy-start | bytes 393220
  28.8 25.2 %collective-permute-start.2 = (bf16[112,256]{1,0:T(8,128)(2,1)S(1)}, bf16[112,256]{1,0:T(8,128)(2,1)S(1)}, u32[]{:S(2)}, u32[]{:S(2)}) collective-permute-start(bf16[112,256]{1,0:T(8,128)(2,1)S(1)} %get-tuple-element.39.own), channel_id=1, source_target_pairs={{0,1},{1,0},{2,3},{3,2},{4,5},{5,4},{6,7},{7,6},{8,9},{9,8},{10,11... | collective-permute-start | bytes 172040 | tf_op jit(solution)/shard_map/ppermute | solution.py:467
  28.8 1.3 %copy-start.11 = (bf16[16,256,128]{2,1,0:T(8,128)(2,1)S(1)}, bf16[16,256,128]{2,1,0:T(8,128)(2,1)}, u32[]{:S(2)}) copy-start(bf16[16,256,128]{2,1,0:T(8,128)(2,1)} %copy-done.10) | copy-start | bytes 3145732
  30.1 1.2 %copy-start.16 = (bf16[16,128,256]{2,1,0:T(8,128)(2,1)S(1)}, bf16[16,128,256]{2,1,0:T(8,128)(2,1)}, u32[]{:S(2)}) copy-start(bf16[16,128,256]{2,1,0:T(8,128)(2,1)} %copy-done.15) | copy-start | bytes 3145732
  36.7 4.5 %copy-start.9 = (s32[8,8]{1,0:T(8,128)S(1)}, s32[8,8]{1,0:T(8,128)}, u32[]{:S(2)}) copy-start(s32[8,8]{1,0:T(8,128)} %far.1) | copy-start | bytes 772
  36.7 4.5 %copy-start.24 = (bf16[8,128,256]{2,1,0:T(8,128)(2,1)S(1)}, bf16[8,128,256]{2,1,0:T(8,128)(2,1)}, u32[]{:S(2)}) copy-start(bf16[8,128,256]{2,1,0:T(8,128)(2,1)} %copy-done.23) | copy-start | bytes 1572868
  36.7 4.5 %copy-start.26 = (bf16[8,256,128]{2,1,0:T(8,128)(2,1)S(1)}, bf16[8,256,128]{2,1,0:T(8,128)(2,1)}, u32[]{:S(2)}) copy-start(bf16[8,256,128]{2,1,0:T(8,128)(2,1)} %copy-done.25) | copy-start | bytes 1572868
  41.2 7.5 %copy-start.19 = (f32[4,32,256]{2,1,0:T(8,128)}, f32[4,32,256]{2,1,0:T(8,128)S(1)}, u32[]{:S(2)}) copy-start(f32[4,32,256]{2,1,0:T(8,128)S(1)} %shard_map.97.rest_2_) | copy-start | bytes 393220
  41.3 0.9 copy-start.28
  42.2 6.6 %copy-start.12 = (bf16[16,256,128]{2,1,0:T(8,128)(2,1)S(1)}, bf16[16,256,128]{2,1,0:T(8,128)(2,1)}, u32[]{:S(2)}) copy-start(bf16[16,256,128]{2,1,0:T(8,128)(2,1)} %copy-done.10) | copy-start | bytes 3145732
  42.2 6.6 %copy-start.17 = (bf16[16,128,256]{2,1,0:T(8,128)(2,1)S(1)}, bf16[16,128,256]{2,1,0:T(8,128)(2,1)}, u32[]{:S(2)}) copy-start(bf16[16,128,256]{2,1,0:T(8,128)(2,1)} %copy-done.15) | copy-start | bytes 3145732
  48.7 5.3 %copy-start.4 = (s32[30,256]{1,0:T(8,128)S(1)}, s32[30,256]{1,0:T(8,128)}, u32[]{:S(2)}) copy-start(s32[30,256]{1,0:T(8,128)} %skel.9) | copy-start | bytes 92164
  55.4 4.2 %collective-permute-start.3 = (bf16[112,256]{1,0:T(8,128)(2,1)S(1)}, bf16[112,256]{1,0:T(8,128)(2,1)S(1)}, u32[]{:S(2)}, u32[]{:S(2)}) collective-permute-start(bf16[112,256]{1,0:T(8,128)(2,1)S(1)} %get-tuple-element.41.own), channel_id=1, source_target_pairs={{0,2},{1,3},{2,0},{3,1},{4,6},{5,7},{6,4},{7,5},{8,10},{9,11},{10,... | collective-permute-start | bytes 172040 | tf_op jit(solution)/shard_map/ppermute | solution.py:467
  60.9 4.2 %collective-permute-start.4 = (bf16[112,256]{1,0:T(8,128)(2,1)S(1)}, bf16[112,256]{1,0:T(8,128)(2,1)S(1)}, u32[]{:S(2)}, u32[]{:S(2)}) collective-permute-start(bf16[112,256]{1,0:T(8,128)(2,1)S(1)} %get-tuple-element.44.own), channel_id=1, source_target_pairs={{0,4},{1,5},{2,6},{3,7},{4,0},{5,1},{6,2},{7,3},{8,12},{9,13},{10,... | collective-permute-start | bytes 172040 | tf_op jit(solution)/shard_map/ppermute | solution.py:467
  66.4 4.2 %collective-permute-start.5 = (bf16[112,256]{1,0:T(8,128)(2,1)S(1)}, bf16[112,256]{1,0:T(8,128)(2,1)S(1)}, u32[]{:S(2)}, u32[]{:S(2)}) collective-permute-start(bf16[112,256]{1,0:T(8,128)(2,1)S(1)} %get-tuple-element.47.own), channel_id=1, source_target_pairs={{0,8},{1,9},{2,10},{3,11},{4,12},{5,13},{6,14},{7,15},{8,0},{9,1},... | collective-permute-start | bytes 172040 | tf_op jit(solution)/shard_map/ppermute | solution.py:467
  71.9 10.0 %copy-start.1 = (bf16[15,256,512]{2,1,0:T(8,128)(2,1)S(1)}, bf16[15,256,512]{2,1,0:T(8,128)(2,1)}, u32[]{:S(2)}) copy-start(bf16[15,256,512]{2,1,0:T(8,128)(2,1)} %copy-done) | copy-start | bytes 11796484
  71.9 9.6 %collective-permute-start.6 = (bf16[112,256]{1,0:T(8,128)(2,1)S(1)}, bf16[112,256]{1,0:T(8,128)(2,1)S(1)}, u32[]{:S(2)}, u32[]{:S(2)}) collective-permute-start(bf16[112,256]{1,0:T(8,128)(2,1)S(1)} %get-tuple-element.50), channel_id=1, source_target_pairs={{0,16},{1,17},{2,18},{3,19},{4,20},{5,21},{6,22},{7,23},{8,24},{9,... | collective-permute-start | bytes 172040 | tf_op jit(solution)/shard_map/ppermute | solution.py:467
  74.6 1.2 %copy-start.13 = (bf16[16,256,128]{2,1,0:T(8,128)(2,1)S(1)}, bf16[16,256,128]{2,1,0:T(8,128)(2,1)}, u32[]{:S(2)}) copy-start(bf16[16,256,128]{2,1,0:T(8,128)(2,1)} %copy-done.10) | copy-start | bytes 3145732
  75.8 1.2 %copy-start.18 = (bf16[16,128,256]{2,1,0:T(8,128)(2,1)S(1)}, bf16[16,128,256]{2,1,0:T(8,128)(2,1)}, u32[]{:S(2)}) copy-start(bf16[16,128,256]{2,1,0:T(8,128)(2,1)} %copy-done.15) | copy-start | bytes 3145732
  81.5 2.8 %copy-start.7 = (s32[1,4096]{1,0:T(1,128)S(1)}, s32[1,4096]{1,0:T(1,128)}, u32[]{:S(2)}) copy-start(s32[1,4096]{1,0:T(1,128)} %order.3) | copy-start | bytes 49156
  81.5 2.8 %copy-start.14 = (bf16[16,256,128]{2,1,0:T(8,128)(2,1)S(1)}, bf16[16,256,128]{2,1,0:T(8,128)(2,1)}, u32[]{:S(2)}) copy-start(bf16[16,256,128]{2,1,0:T(8,128)(2,1)} %copy-done.10) | copy-start | bytes 3145732
  81.5 2.8 %copy-start.20 = (f32[4,32,256]{2,1,0:T(8,128)S(1)}, f32[4,32,256]{2,1,0:T(8,128)}, u32[]{:S(2)}) copy-start(f32[4,32,256]{2,1,0:T(8,128)} %copy-done.19) | copy-start | bytes 393220
  81.5 2.8 %copy-start.22 = (f32[4,32,256]{2,1,0:T(8,128)S(1)}, f32[4,32,256]{2,1,0:T(8,128)}, u32[]{:S(2)}) copy-start(f32[4,32,256]{2,1,0:T(8,128)} %copy-done.21) | copy-start | bytes 393220
  (4 other events, 3.0 us)
where the time goes:
time: 106 us; the launch traced here: 105 us
  Pallas kernels  66.4 us (63%)
  local copies, waits for them, and re-layouts  14.7 us (14%)
  waiting for transfers between devices  12.3 us (12%)
  starting transfers between devices  10.2 us (10%)
    pallas_call x1, Pallas kernels, local(): call(functools.partial(final_kernel, kern_scale, features), shape((rhs, t...  20.6 us
    pallas_call x4, Pallas kernels, local(): call(functools.partial(near_own_kernel, kern_scale, cuts[k]), shape((coun...  18.8 us
    unnamed x58, local copies, waits for them, and re-layouts  14.7 us
    ppermute x5, waiting for transfers between devices, local(): lax.ppermute(own, 'leaf', [(i, i ^ 1 << bit) for i in range(devices)])  12.3 us
    pallas_call x1, Pallas kernels, local(): call(gather_kernel, shape((rows, total), BF), [VMEM] * 3, [pltpu.VMEM((le...  6.73 us
    pallas_call x1, Pallas kernels, local(): call(functools.partial(far_kernel, kern_scale), shape((half, rhs, width),...  6.53 us
    pallas_call x1, Pallas kernels, local(): call(functools.partial(tree_kernel, kern_scale, features), (shape((leaves...  5.9 us
    ppermute x1, starting transfers between devices, local(): right = lax.ppermute(stacked, 'leaf', [(i + 1, i) for i in ring])  5.44 us
  transfers between devices with their start and end apart: 7, of which 3 were waited for; matrix products, arithmetic and copies ran while one was open for 0% of the time, Pallas kernels for 37%

commit v1 on v0

v1 whole, which is shorter than its diff:
```python
import functools
import math

import jax
import jax.numpy as jnp
from jax import lax
from jax.experimental import pallas as pl
from jax.experimental.pallas import tpu as pltpu
from jax.sharding import PartitionSpec as P

PAIR_GAIN = math.sqrt(2.0)
LOG2E = math.log2(math.e)
BF = jnp.bfloat16
F32 = jnp.float32
NT = (((1,), (1,)), ((), ()))
AUX = 8
DEPTH = 128
BATCH, SMALL = 24, 8
FILL = 28
FILLERS = 5
UNROLL = 4
VMEM = pl.BlockSpec(memory_space=pltpu.VMEM)
SMEM = pl.BlockSpec(memory_space=pltpu.SMEM)
HBM = pl.BlockSpec(memory_space=pltpu.HBM)
ANY = pl.BlockSpec(memory_space=pl.ANY)


def nt_dot(a, b):
    return lax.dot_general(a, b, NT, preferred_element_type=F32)


def nn_dot(a, b):
    return jnp.dot(a, b, preferred_element_type=F32)


def call(body, out_shape, in_specs, scratch, flops, out_specs=None, aliases=None, limit_mb=16):
    return pl.pallas_call(
        body,
        out_shape=out_shape,
        in_specs=in_specs,
        out_specs=out_specs or jax.tree.map(lambda _: VMEM, out_shape),
        input_output_aliases=aliases or {},
        scratch_shapes=scratch,
        compiler_params=pltpu.CompilerParams(vmem_limit_bytes=limit_mb * 2**20),
        cost_estimate=pl.CostEstimate(flops=flops, bytes_accessed=2**20, transcendentals=0),
    )


def kernel_tile(sq_dist, kern_scale):
    floor = jnp.maximum(sq_dist, 1e-30)
    root = floor * lax.rsqrt(floor)
    decay = jnp.exp2(root * (-kern_scale * LOG2E))
    return ((1.0 + root * kern_scale) * decay).astype(BF)


def aux_rows(x):
    width = x.shape[1]
    norm = jnp.sum(x * x, axis=0, keepdims=True)
    high = norm.astype(BF).astype(F32)
    rest = norm - high
    mid = rest.astype(BF).astype(F32)
    low = rest - mid
    row = lax.broadcasted_iota(jnp.int32, (AUX, width), 0)
    norms = jnp.where(row == 0, high, jnp.where(row == 1, mid, jnp.where(row == 2, low, 0.0)))
    ones = jnp.where(row < 3, 1.0, 0.0)
    return norms, ones


def source_form(x, norms, ones):
    pad = jnp.zeros((DEPTH - x.shape[0] - 2 * AUX, x.shape[1]), F32)
    return jnp.concatenate([x, norms, ones, pad], axis=0).astype(BF)


def target_form(x, norms, ones):
    pad = jnp.zeros((DEPTH - x.shape[0] - 2 * AUX, x.shape[1]), F32)
    return jnp.concatenate([-2.0 * x, ones, norms, pad], axis=0).T.astype(BF)


def split_form(selected, features):
    return (
        selected[:features],
        selected[features : features + AUX],
        selected[features + AUX : features + 2 * AUX],
    )


def one_hot(chosen, height):
    width = chosen.shape[1]
    row = lax.broadcasted_iota(jnp.int32, (height, width), 0)
    return jnp.where(row == chosen, 1.0, 0.0).astype(BF)


def flat(table, size):
    rows, cols = table.shape
    entry = lax.broadcasted_iota(jnp.int32, (cols, size), 1)
    pick = jnp.where(entry % cols == lax.broadcasted_iota(jnp.int32, (cols, size), 0), 1.0, 0.0)
    every = nn_dot(table.astype(BF), pick.astype(BF))
    entry = lax.broadcasted_iota(jnp.int32, (rows, size), 1)
    row = lax.broadcasted_iota(jnp.int32, (rows, size), 0)
    return jnp.sum(jnp.where(entry // cols == row, every, 0.0), axis=0, keepdims=True)


def pair_list(near, far, first_leaf, length, fixed):
    leaves, slots = near.shape
    nodes, _ = far.shape
    upper = nodes - 2
    near_size, far_size = leaves * slots, nodes * nodes
    size = -(-(near_size + far_size + upper) // 128) * 128
    rest = size - near_size - far_size
    row = lax.broadcasted_iota(jnp.int32, (nodes, nodes), 0)
    col = lax.broadcasted_iota(jnp.int32, (nodes, nodes), 1)
    seen = jnp.where(col == row + 1 - 2 * (row & 1), 1.0, 0.0)
    for s in range(far.shape[1]):
        seen = seen + jnp.where(far[:, s : s + 1] == col, 1.0, 0.0)
    here = jnp.where(near >= 0, near - (first_leaf - leaves), -1).astype(F32)
    column = lax.broadcasted_iota(jnp.int32, (1, size), 1)
    is_far = (column >= near_size) & (column < near_size + far_size)
    is_up = (column >= near_size + far_size) & (column < near_size + far_size + upper)
    near_h = jnp.concatenate([flat(here, near_size), jnp.full((1, size - near_size), -1.0, F32)], axis=1)
    times = jnp.concatenate(
        [jnp.zeros((1, near_size), F32), flat(seen, far_size + rest)], axis=1
    )
    from_far = column - near_size
    from_up = from_far - far_size
    node_first = 2 * leaves
    up_at = nodes + from_up
    sibling = up_at + 1 - 2 * (from_up & 1)
    source = jnp.where(
        is_far, node_first + from_far % nodes, jnp.where(is_up, node_first + sibling, 0)
    ).astype(F32) + jnp.where(column < near_size, near_h, 0.0)
    target = jnp.where(
        is_far, leaves + from_far // nodes, jnp.where(is_up, leaves + up_at, column // slots)
    ).astype(F32)
    times = jnp.where(is_far, times, jnp.where(is_up | (near_h >= 0), 1.0, 0.0))
    level = jnp.where(times > 0, 1.0, 0.0)
    first = jnp.where(is_far | is_up, level, 0.0)
    own = jnp.where((near_h >= leaves) & (near_h < 2 * leaves), 1.0, 0.0)
    other = level - first - own
    row = lax.broadcasted_iota(jnp.int32, (16, size), 0)
    masks = jnp.where(row == 0, first, jnp.where(row == 1, own, jnp.where(row == 2, other, 0.0)))
    before = lax.broadcasted_iota(jnp.int32, (size, size), 1) < lax.broadcasted_iota(
        jnp.int32, (size, size), 0
    )
    rank = nt_dot(masks.astype(BF), jnp.where(before, 1.0, 0.0).astype(BF))
    found = jnp.sum(masks, axis=1, keepdims=True)
    start = jnp.maximum(found[0:1] + found[1:2], float(fixed))
    place = jnp.where(other > 0, start + rank[2:3], -1.0)
    place = jnp.where(own > 0, found[0:1] + rank[1:2], place)
    place = jnp.where(first > 0, rank[0:1], place)
    slot = lax.broadcasted_iota(jnp.int32, (length, size), 0).astype(F32)
    hit = jnp.where(slot == place, 1.0, 0.0).astype(BF)
    parts = jnp.where(row == 0, source, jnp.where(row == 1, target, jnp.where(row == 2, times, 0.0)))
    listed = nt_dot(parts.astype(BF), hit)
    code = (listed[0:1] + 256.0 * listed[1:2] + 65536.0 * listed[2:3]).astype(jnp.int32)
    code = jnp.where(listed[2:3] > 0.5, code, leaves)
    total = jnp.broadcast_to(start + found[2:3], (1, length)).astype(jnp.int32)
    return jnp.concatenate([code, total], axis=0)


def gather_kernel(
    fixed, points, charges, order, near, far, place, stacked, pairs, grid, hots, index, slots, far_slots, sems
):
    features, total = points.shape
    rows = stacked.shape[0]
    width = hots.shape[1]
    blocks = grid.shape[0]
    fetch_index = pltpu.make_async_copy(order, index, sems.at[2 * blocks])
    fetch_index.start()
    fetches = []
    for b in range(blocks):
        cols = pl.ds(b * width, width)
        into = grid.at[b, pl.ds(0, features)]
        fetches.append(pltpu.make_async_copy(points.at[:, cols], into, sems.at[2 * b]))
        into = grid.at[b, pl.ds(features, rows - features)]
        fetches.append(pltpu.make_async_copy(charges.at[:, cols], into, sems.at[2 * b + 1]))
    fetch_slots = pltpu.make_async_copy(near, slots, sems.at[2 * blocks + 1])
    fetch_slots.start()
    fetch_far = pltpu.make_async_copy(far, far_slots, sems.at[2 * blocks + 2])
    fetch_far.start()
    for fetch in fetches:
        fetch.start()
    fetch_index.wait()
    for b in range(blocks):
        hots[b] = one_hot(index[:, pl.ds(b * width, width)] & (width - 1), width)
    fetch_slots.wait()
    fetch_far.wait()
    pairs[...] = pair_list(slots[...], far_slots[...], place[0] * blocks, pairs.shape[1], fixed)
    for fetch in fetches:
        fetch.wait()

    def block(i, carry):
        for u in range(UNROLL):
            j = i * UNROLL + u
            start = pl.multiple_of(j * width, width)
            home = index[:, pl.ds(start, width)] // width
            spread = nn_dot(grid[...].reshape(blocks * rows, width), hots[j])
            found = spread[:rows]
            for b in range(1, blocks):
                found = jnp.where(home == b, spread[b * rows : (b + 1) * rows], found)
            stacked[:, pl.ds(start, width)] = found.astype(BF)
        return carry

    lax.fori_loop(0, blocks // UNROLL, block, 0)


def lift(sources, weights, target, kern_scale):
    kernel = kernel_tile(nn_dot(target, sources), kern_scale)
    sums = nt_dot(weights, kernel)
    rhs = weights.shape[0] - 16
    lifted = PAIR_GAIN * (sums[:rhs] / sums[rhs : rhs + 1])
    return kernel, lifted


def with_ones(weights):
    return jnp.concatenate([weights, jnp.ones((16, weights.shape[1]), weights.dtype)], axis=0)


def tree_kernel(
    kern_scale, features, stacked, skel, srcs, tgts, wtss, kernels, payload, top_tgt, joined, joined_w,
):
    width = skel.shape[1]
    nodes = skel.shape[0]
    leaves = nodes + 1
    for leaf in range(leaves):
        cols = pl.ds(leaf * width, width)
        x = stacked[:features, cols].astype(F32)
        norms, ones = aux_rows(x)
        srcs[leaf] = source_form(x, norms, ones)
        tgts[leaf] = target_form(x, norms, ones)
        wtss[leaf] = stacked[features:, cols]
    live = features + 2 * AUX
    for row in range(nodes):
        slot = row % 8
        for side in range(2):
            joined[slot, :, side * width : (side + 1) * width] = srcs[2 * row + side]
            joined_w[slot, :, side * width : (side + 1) * width] = with_ones(wtss[2 * row + side])
        hot = one_hot(skel[row : row + 1, :], 2 * width)
        x, norms, ones = split_form(nn_dot(joined[slot, :live], hot), features)
        own_src = source_form(x, norms, ones)
        own_tgt = target_form(x, norms, ones)
        kernel, lifted = lift(joined[slot], joined_w[slot], own_tgt, kern_scale)
        kernels[row] = kernel
        own_wts = lifted.astype(BF)
        if row < nodes - 1:
            srcs[leaves + row], tgts[leaves + row], wtss[leaves + row] = own_src, own_tgt, own_wts
        else:
            payload[:live] = own_src[:live]
            payload[live:] = own_wts
            top_tgt[...] = own_tgt


def padded(rows):
    return jnp.concatenate(
        [rows, jnp.zeros((DEPTH - rows.shape[0], rows.shape[1]), rows.dtype)], axis=0
    )


def chain_kernel(
    kern_scale, features, bit, devices, place, own, sibling, skel, _, next_own, next_tgt, half_kernel, joined, joined_w
):
    live = features + 2 * AUX
    width = own.shape[1]
    joined[:, :width] = padded(own[:live])
    joined[:, width:] = padded(sibling[:live])
    joined_w[:, :width] = with_ones(own[live:])
    joined_w[:, width:] = with_ones(sibling[live:])
    chosen = skel[pl.ds(devices - (devices >> bit) + (place[0] >> (bit + 1)), 1), :]
    chosen = chosen + ((place[0] >> bit) & 1) * jnp.where(chosen < width, width, -width)
    hot = one_hot(chosen, 2 * width)
    x, norms, ones = split_form(nn_dot(joined[:live], hot), features)
    target = target_form(x, norms, ones)
    kernel, lifted = lift(joined[...], joined_w[...], target, kern_scale)
    half_kernel[...] = kernel[:, :width]
    next_tgt[...] = target
    next_own[:live] = source_form(x, norms, ones)[:live]
    next_own[live:] = lifted.astype(BF)


def pair_terms(kern_scale, codes, src, tgt, wts, acc, first=0):
    terms = []
    for code in codes:
        h = (code & 255) - first
        g = (code >> 8) & 255
        times = (code >> 16).astype(F32)
        kernel = kernel_tile(nn_dot(tgt[g], src[h]), kern_scale)
        terms.append((g, nt_dot(wts[h], kernel) * times))
    for g, term in terms:
        acc[g] = acc[g] + term


def pair_loop(total, batch):
    large = total // BATCH

    def step(i, carry):
        batch(i * BATCH, BATCH)
        return carry

    def small_step(i, carry):
        batch(large * BATCH + i * SMALL, SMALL)
        return carry

    lax.fori_loop(0, large, step, 0)
    lax.fori_loop(0, (total - large * BATCH + (SMALL - 1)) // SMALL, small_step, 0)


def own_kernel(kern_scale, part, pairs, src, tgt, wts, _, *rest):
    acc = rest[-1]
    if part == 0:
        acc[...] = jnp.zeros_like(acc)
    codes = [pairs[0, part * FILL + u] for u in range(FILL)]
    pair_terms(kern_scale, codes, src, tgt, wts, acc, (src.shape[0] + 2) // 2)


def down_kernel(kern_scale, upper, live, kernels, acc, *rest):
    siblings = rest[:upper]
    targets = rest[upper : 2 * upper]
    half_kernels = rest[2 * upper : 3 * upper - 1]
    root, leaf_field = rest[3 * upper - 1 :]
    width = root.shape[1]
    nodes = kernels.shape[0]
    leaves = nodes + 1
    rhs = root.shape[0]

    def push(field, kernel):
        sums = nn_dot(with_ones(field.astype(BF)), kernel)
        return sums[:rhs] / sums[rhs : rhs + 1]

    coupled = []
    for bit in range(upper):
        kernel = kernel_tile(nn_dot(targets[bit][...], padded(siblings[bit][:live])), kern_scale)
        coupled.append(nt_dot(siblings[bit][live:], kernel))
    field = coupled[upper - 1]
    for bit in range(upper - 2, -1, -1):
        field = coupled[bit] + push(field, half_kernels[bit][...])
    root[...] = field
    fields = {nodes - 1: field}
    for row in range(nodes - 1, -1, -1):
        pushed = push(fields[row], kernels[row])
        for side in range(2):
            below = 2 * row + side
            passed = pushed[:, side * width : (side + 1) * width]
            if below < leaves:
                leaf_field[below] = passed
            else:
                fields[below - leaves] = acc[below] + passed


def final_kernel(
    kern_scale, features, fixed, pairs, left, right, own_src, own_wts, tgt, order, leaf_field, own_acc,
    out, src, wts, acc, spread,
):
    leaves = leaf_field.shape[0]
    width = leaf_field.shape[2]
    rhs = out.shape[0]
    for side, halo in ((0, left), (2, right)):
        for leaf in range(leaves):
            cols = pl.ds(leaf * width, width)
            x = halo[:features, cols].astype(F32)
            src[side * leaves + leaf] = source_form(x, *aux_rows(x))
            wts[side * leaves + leaf] = halo[features:, cols]
    src[pl.ds(leaves, leaves)] = own_src[pl.ds(0, leaves)]
    wts[pl.ds(leaves, leaves)] = own_wts[pl.ds(0, leaves)]
    acc[...] = own_acc[pl.ds(0, leaves)] + leaf_field[...]

    def batch(first, size):
        codes = [pairs[0, fixed + first + u] for u in range(size)]
        pair_terms(kern_scale, codes, src, tgt, wts, acc)

    pair_loop(pairs[1, 0] - fixed, batch)
    spread[...] = jnp.zeros_like(spread)
    span = UNROLL * width

    def scatter(i, carry):
        index = order[:, pl.ds(pl.multiple_of(i * span, span), span)]
        home = index // width
        hot_t = one_hot(index & (width - 1), width)
        rows = jnp.concatenate([acc[i * UNROLL + u] for u in range(UNROLL)], axis=1)
        high = rows.astype(BF)
        low = (rows - high.astype(F32)).astype(BF)
        both = jnp.concatenate([high, low], axis=0)
        stack = []
        for b in range(leaves):
            mask = jnp.where(home == b, 1.0, 0.0).astype(BF)
            stack.append(both * mask)
        spread[...] += nt_dot(jnp.concatenate(stack, axis=0), hot_t)
        return carry

    lax.fori_loop(0, leaves // UNROLL, scatter, 0)
    for b in range(leaves):
        at = b * 2 * rhs
        out[:, pl.ds(b * width, width)] = spread[pl.ds(at, rhs)] + spread[pl.ds(at + rhs, rhs)]


def local(points, charges, leaf_order, near_list, far_list, local_skel, upper_skel):
    features, total = points.shape
    rhs = charges.shape[0]
    leaves, _ = near_list.shape
    width = local_skel.shape[1]
    nodes = local_skel.shape[0]
    kern_scale = 2.0 * math.sqrt(3.0 / features)
    devices = lax.axis_size("leaf")
    upper = devices.bit_length() - 1
    depth = leaves.bit_length() - 1
    position = lax.axis_index("leaf")
    live = features + 2 * AUX
    rows = features + rhs
    shape = jax.ShapeDtypeStruct
    place = jnp.reshape(position, (1,)).astype(jnp.int32)

    half = leaves // 2
    fillers = min(FILLERS, upper)
    fixed = fillers * FILL
    pairs_most = near_list.size + half * half + half - 2
    length = -(-(max(pairs_most, near_list.size + fixed) + BATCH) // 128) * 128
    stacked, pairs = call(
        functools.partial(gather_kernel, fixed),
        (shape((rows, total), BF), shape((2, length), jnp.int32)),
        [HBM] * 5 + [SMEM],
        [
            pltpu.VMEM((leaves, rows, width), BF),
            pltpu.VMEM((leaves, width, width), BF),
            pltpu.VMEM((1, total), jnp.int32),
            pltpu.VMEM(near_list.shape, jnp.int32),
            pltpu.VMEM(far_list.shape, jnp.int32),
            pltpu.SemaphoreType.DMA((2 * leaves + 3,)),
        ],
        10**10,
        limit_mb=63,
    )(points, charges, leaf_order, near_list, far_list, place)
    ring = list(range(devices - 1))
    left = lax.ppermute(stacked, "leaf", [(i, i + 1) for i in ring])
    right = lax.ppermute(stacked, "leaf", [(i + 1, i) for i in ring])

    known = leaves + nodes - 1
    srcs, tgts, wtss, kernels, own, own_tgt = call(
        functools.partial(tree_kernel, kern_scale, features),
        (
            shape((known, DEPTH, width), BF),
            shape((known, width, DEPTH), BF),
            shape((known, rhs, width), BF),
            shape((nodes, width, 2 * width), BF),
            shape((live + rhs, width), BF),
            shape((width, DEPTH), BF),
        ),
        [VMEM] * 2,
        [pltpu.VMEM((8, DEPTH, 2 * width), BF), pltpu.VMEM((8, rhs + 16, 2 * width), BF)],
        10**10,
    )(stacked, local_skel)

    siblings, targets, half_kernels = [], [], []
    acc = None
    for bit in range(upper):
        sibling = lax.ppermute(own, "leaf", [(i, i ^ (1 << bit)) for i in range(devices)])
        if bit < fillers:
            acc = call(
                functools.partial(own_kernel, kern_scale, bit),
                shape((known, rhs, width), F32),
                [SMEM] + [VMEM] * 3 + [ANY] + [VMEM] * (bit > 0),
                [],
                4 * 10**9,
                aliases={5: 0} if bit else None,
            )(pairs, srcs, tgts, wtss, own, *([acc] if bit else []))
        siblings.append(sibling)
        targets.append(own_tgt)
        if bit == upper - 1:
            break
        own, own_tgt, half_kernel = call(
            functools.partial(chain_kernel, kern_scale, features, bit, devices),
            (
                shape((live + rhs, width), BF),
                shape((width, DEPTH), BF),
                shape((width, width), BF),
            ),
            [SMEM] + [VMEM] * 3 + [ANY],
            [pltpu.VMEM((DEPTH, 2 * width), BF), pltpu.VMEM((rhs + 16, 2 * width), BF)],
            10**8,
        )(place, own, sibling, upper_skel, acc)
        half_kernels.append(half_kernel)

    root, leaf_field = call(
        functools.partial(down_kernel, kern_scale, upper, live),
        (shape((rhs, width), F32), shape((leaves, rhs, width), F32)),
        [VMEM] * (2 + 3 * upper - 1),
        [],
        10**9,
    )(kernels, acc, *siblings, *targets, *half_kernels)

    potentials = call(
        functools.partial(final_kernel, kern_scale, features, fixed),
        shape((rhs, total), F32),
        [SMEM] + [VMEM] * 8,
        [
            pltpu.VMEM((3 * leaves, DEPTH, width), BF),
            pltpu.VMEM((3 * leaves, rhs, width), BF),
            pltpu.VMEM((leaves, rhs, width), F32),
            pltpu.VMEM((leaves * 2 * rhs, width), F32),
        ],
        10**10,
    )(pairs, left, right, srcs, wtss, tgts, leaf_order, leaf_field, acc)
    return (potentials, root[None])


def solution(mesh):
    placed = (
        P(None, "leaf"),
        P(None, "leaf"),
        P("leaf", None),
        P("leaf", None),
        P("leaf", None),
        P("leaf", None),
        P(),
    )
    return jax.shard_map(
        local,
        mesh=mesh,
        in_specs=placed,
        out_specs=(P(None, "leaf"), P("leaf", None, None)),
        check_vma=False,
    )
```

time: 106 us -> 70.4 us (0.66)
  local copies, waits for them, and re-layouts: 14.7 us -> 1.15 us
  Pallas kernels: 66.4 us -> 53.5 us
  waiting for transfers between devices: 12.3 us -> 3.16 us
  starting transfers between devices: 10.2 us -> 11.7 us
    unnamed x58 -> x10, local copies, waits for them, and re-layouts: 14.7 us -> 1.15 us
    pallas_call x14 -> x13, Pallas kernels: 66.4 us -> 53.5 us  [the longest x1 19.1 us: local(): call(functools.partial(final_kernel, kern_scale, features, fixed), shape(...]
    ppermute x5, waiting for transfers between devices: 12.3 us -> 3.15 us  [local(): lax.ppermute(own, 'leaf', [(i, i ^ 1 << bit) for i in range(devices)])]
    ppermute x5, starting transfers between devices: 2.87 us -> 4.33 us  [local(): lax.ppermute(own, 'leaf', [(i, i ^ 1 << bit) for i in range(devices)])]
  transfers between devices with their start and end apart: 7 -> 7, of which waited for: 3 -> 2; matrix products, arithmetic and copies ran while one was open for 0% -> 0% of each run, Pallas kernels for 37% -> 39%
where the time goes in v1:
time: 70.4 us
  Pallas kernels  53.5 us (76%)
  starting transfers between devices  11.7 us (17%)
  waiting for transfers between devices  3.16 us (4%)
  local copies, waits for them, and re-layouts  1.15 us (2%)
  between operations  0.85 us (1%)
    pallas_call x1, Pallas kernels, local(): call(functools.partial(final_kernel, kern_scale, features, fixed), shape(...  19.1 us
    pallas_call x5, Pallas kernels, local(): call(functools.partial(own_kernel, kern_scale, bit), shape((known, rhs, w...  16.4 us
    pallas_call x1, Pallas kernels, local(): call(functools.partial(gather_kernel, fixed), (shape((rows, total), BF),...  6.9 us
    pallas_call x1, Pallas kernels, local(): call(functools.partial(tree_kernel, kern_scale, features), (shape((known,...  5.92 us
    ppermute x1, starting transfers between devices, local(): right = lax.ppermute(stacked, 'leaf', [(i + 1, i) for i in ring])  5.44 us
    ppermute x5, starting transfers between devices, local(): lax.ppermute(own, 'leaf', [(i, i ^ 1 << bit) for i in range(devices)])  4.33 us
    ppermute x5, waiting for transfers between devices, local(): lax.ppermute(own, 'leaf', [(i, i ^ 1 << bit) for i in range(devices)])  3.15 us
    pallas_call x4, Pallas kernels, local(): call(functools.partial(chain_kernel, kern_scale, features, bit, devices),...  2.81 us
  transfers between devices with their start and end apart: 7, of which 2 were waited for; matrix products, arithmetic and copies ran while one was open for 0% of the time, Pallas kernels for 39%

profile of v1, /device:TPU:8, one launch (start us, length us, event | category | flops | bytes accessed | tf_op | source)
XLA Modules:
  0.0 70.4 jit_solution(13274509615509784142)
XLA Ops:
  0.6 0.0 copy-start.2
  0.6 6.9 %shard_map.86 = (bf16[96,4096]{1,0:T(8,128)(2,1)}, s32[2,512]{1,0:T(2,128)}) custom-call(bf16[64,4096]{1,0:T(8,128)(2,1)} %points.1, bf16[32,4096]{1,0:T(8,128)(2,1)} %charges.1, s32[1,4096]{1,0:T(1,128)} %order.3, s32[16,16]{1,0:T(8,128)} %near.1, s32[8,8]{1,0:T(8,128)} %far.1, s32[1]{0:T(128)} %bitcast.place), custom_call_target="tpu_custom_call" | custom-call | flops 10000000000 | bytes 1048576 | tf_op jit(solution)/shard_map/pallas_call | solution.py:415
  7.6 1.9 %collective-permute-start = (bf16[96,4096]{1,0:T(8,128)(2,1)}, bf16[96,4096]{1,0:T(8,128)(2,1)S(1)}, u32[]{:S(2)}, u32[]{:S(2)}) collective-permute-start(bf16[96,4096]{1,0:T(8,128)(2,1)} %get-tuple-element.25.stacked), channel_id=1, source_target_pairs={{0,1},{1,2},{2,3},{3,4},{4,5},{5,6},{6,7},{7,8},{8,9},{9,10},{10,1... | collective-permute-start | bytes 2359304 | tf_op jit(solution)/shard_map/ppermute | solution.py:431
  9.5 5.4 %collective-permute-start.1 = (bf16[96,4096]{1,0:T(8,128)(2,1)}, bf16[96,4096]{1,0:T(8,128)(2,1)S(1)}, u32[]{:S(2)}, u32[]{:S(2)}) collective-permute-start(bf16[96,4096]{1,0:T(8,128)(2,1)} %get-tuple-element.25.stacked), channel_id=1, source_target_pairs={{1,0},{2,1},{3,2},{4,3},{5,4},{6,5},{7,6},{8,7},{9,8},{10,9},{11,1... | collective-permute-start | bytes 2359304 | tf_op jit(solution)/shard_map/ppermute | solution.py:432
  14.9 0.0 copy-done.2
  14.9 1.1 %copy-done.1 = bf16[96,4096]{1,0:T(8,128)(2,1)S(1)} copy-done((bf16[96,4096]{1,0:T(8,128)(2,1)S(1)}, bf16[96,4096]{1,0:T(8,128)(2,1)}, u32[]{:S(2)}) %copy-start.1) | copy-done | bytes 786456
  16.1 5.9 %shard_map.87 = (bf16[30,128,256]{2,1,0:T(8,128)(2,1)S(1)}, bf16[30,256,128]{2,1,0:T(8,128)(2,1)S(1)}, bf16[30,32,256]{2,1,0:T(8,128)(2,1)S(1)}, bf16[15,256,512...) custom-call(bf16[96,4096]{1,0:T(8,128)(2,1)S(1)} %copy-done.1, s32[15,256]{1,0:T(8,128)S(1)} %copy-done.2), custom_call_target="tpu_custom_call" | custom-call | flops 10000000000 | bytes 1048576 | tf_op jit(solution)/shard_map/pallas_call | solution.py:435
  22.0 0.1 collective-permute-start.2
  22.1 0.0 copy-start
  22.1 3.3 %shard_map.88._.rest_0_ = f32[30,32,256]{2,1,0:T(8,128)S(1)} custom-call(s32[2,512]{1,0:T(2,128)S(1)} %copy-done.4, bf16[30,128,256]{2,1,0:T(8,128)(2,1)S(1)} %get-tuple-element.26.src.own_src, bf16[30,256,128]{2,1,0:T(8,128)(2,1)S(1)} %get-tuple-element.28.tgt, bf16[30,32,256]{2,1,0:T(8,128)(2,1)S(1)} %get-tuple-element.27.wts.own_wts, ...), custom_call_target="tpu_custom_call" | custom-call | flops 4000000000 | bytes 1048576 | tf_op jit(solution)/shard_map/pallas_call | solution.py:455
  25.4 0.0 collective-permute-done.2.sibling.rest_0_
  25.4 0.7 shard_map.89
  26.1 0.1 collective-permute-start.3
  26.2 3.2 %shard_map.90._.rest_0_ = f32[30,32,256]{2,1,0:T(8,128)S(1)} custom-call(s32[2,512]{1,0:T(2,128)S(1)} %copy-done.4, bf16[30,128,256]{2,1,0:T(8,128)(2,1)S(1)} %get-tuple-element.26.src.own_src, bf16[30,256,128]{2,1,0:T(8,128)(2,1)S(1)} %get-tuple-element.28.tgt, ...), custom_call_target="tpu_custom_call", output_to_operand_aliasing={{}: (5, {})} | custom-call | flops 4000000000 | bytes 1048576 | tf_op jit(solution)/shard_map/pallas_call | solution.py:455
  29.5 2.2 %collective-permute-done.3.sibling.rest_1_ = bf16[112,256]{1,0:T(8,128)(2,1)S(1)} collective-permute-done((bf16[112,256]{1,0:T(8,128)(2,1)S(1)}, bf16[112,256]{1,0:T(8,128)(2,1)S(1)}, u32[]{:S(2)}, u32[]{:S(2)}) %collective-permute-start.3) | collective-permute-done | bytes 57376 | tf_op jit(solution)/shard_map/ppermute | solution.py:453
  31.7 0.7 shard_map.91
  32.4 1.5 %collective-permute-start.4 = (bf16[112,256]{1,0:T(8,128)(2,1)S(1)}, bf16[112,256]{1,0:T(8,128)(2,1)S(1)}, u32[]{:S(2)}, u32[]{:S(2)}) collective-permute-start(bf16[112,256]{1,0:T(8,128)(2,1)S(1)} %get-tuple-element.32._.own), channel_id=1, source_target_pairs={{0,4},{1,5},{2,6},{3,7},{4,0},{5,1},{6,2},{7,3},{8,12},{9,13},{10,... | collective-permute-start | bytes 172040 | tf_op jit(solution)/shard_map/ppermute | solution.py:453
  33.9 3.4 %shard_map.92._.rest_0_ = f32[30,32,256]{2,1,0:T(8,128)S(1)} custom-call(s32[2,512]{1,0:T(2,128)S(1)} %copy-done.4, bf16[30,128,256]{2,1,0:T(8,128)(2,1)S(1)} %get-tuple-element.26.src.own_src, bf16[30,256,128]{2,1,0:T(8,128)(2,1)S(1)} %get-tuple-element.28.tgt, ...), custom_call_target="tpu_custom_call", output_to_operand_aliasing={{}: (5, {})} | custom-call | flops 4000000000 | bytes 1048576 | tf_op jit(solution)/shard_map/pallas_call | solution.py:455
  37.3 0.0 collective-permute-done.4.sibling.rest_2_
  37.3 0.7 %shard_map.93 = (bf16[112,256]{1,0:T(8,128)(2,1)S(1)}, bf16[256,128]{1,0:T(8,128)(2,1)S(1)}, bf16[256,256]{1,0:T(8,128)(2,1)S(1)}) custom-call(s32[1]{0:T(128)} %bitcast.place, bf16[112,256]{1,0:T(8,128)(2,1)S(1)} %get-tuple-element.32._.own, bf16[112,256]{1,0:T(8,128)(2,1)S(1)} %collective-permute-done.4.sibling.rest_2_, s32[30,256]{1,0:T(8,128)S(1)} %copy-done, ...), custom_call_target="tpu_custom_call" | custom-call | flops 100000000 | bytes 1048576 | tf_op jit(solution)/shard_map/pallas_call | solution.py:467
  38.0 0.1 collective-permute-start.5
  38.1 3.2 %shard_map.94._.rest_0_ = f32[30,32,256]{2,1,0:T(8,128)S(1)} custom-call(s32[2,512]{1,0:T(2,128)S(1)} %copy-done.4, bf16[30,128,256]{2,1,0:T(8,128)(2,1)S(1)} %get-tuple-element.26.src.own_src, bf16[30,256,128]{2,1,0:T(8,128)(2,1)S(1)} %get-tuple-element.28.tgt, ...), custom_call_target="tpu_custom_call", output_to_operand_aliasing={{}: (5, {})} | custom-call | flops 4000000000 | bytes 1048576 | tf_op jit(solution)/shard_map/pallas_call | solution.py:455
  41.3 0.9 %collective-permute-done.5.sibling.rest_3_ = bf16[112,256]{1,0:T(8,128)(2,1)S(1)} collective-permute-done((bf16[112,256]{1,0:T(8,128)(2,1)S(1)}, bf16[112,256]{1,0:T(8,128)(2,1)S(1)}, u32[]{:S(2)}, u32[]{:S(2)}) %collective-permute-start.5) | collective-permute-done | bytes 57376 | tf_op jit(solution)/shard_map/ppermute | solution.py:453
  42.3 0.7 shard_map.95
  43.0 2.6 %collective-permute-start.6 = (bf16[112,256]{1,0:T(8,128)(2,1)S(1)}, bf16[112,256]{1,0:T(8,128)(2,1)S(1)}, u32[]{:S(2)}, u32[]{:S(2)}) collective-permute-start(bf16[112,256]{1,0:T(8,128)(2,1)S(1)} %get-tuple-element.34._), channel_id=1, source_target_pairs={{0,16},{1,17},{2,18},{3,19},{4,20},{5,21},{6,22},{7,23},{8,24},{9,... | collective-permute-start | bytes 172040 | tf_op jit(solution)/shard_map/ppermute | solution.py:453
  45.6 3.2 %shard_map.96.acc.own_acc = f32[30,32,256]{2,1,0:T(8,128)S(1)} custom-call(s32[2,512]{1,0:T(2,128)S(1)} %copy-done.4, bf16[30,128,256]{2,1,0:T(8,128)(2,1)S(1)} %get-tuple-element.26.src.own_src, bf16[30,256,128]{2,1,0:T(8,128)(2,1)S(1)} %get-tuple-element.28.tgt, ...), custom_call_target="tpu_custom_call", output_to_operand_aliasing={{}: (5, {})} | custom-call | flops 4000000000 | bytes 1048576 | tf_op jit(solution)/shard_map/pallas_call | solution.py:455
  48.9 0.0 collective-permute-done.6.rest_4_
  48.9 0.0 copy-start.3
  48.9 2.3 %shard_map.97 = (f32[32,256]{1,0:T(8,128)}, f32[16,32,256]{2,1,0:T(8,128)S(1)}) custom-call(bf16[15,256,512]{2,1,0:T(8,128)(2,1)S(1)} %get-tuple-element.29.kernels, f32[30,32,256]{2,1,0:T(8,128)S(1)} %shard_map.96.acc.own_acc, bf16[112,256]{1,0:T(8,128)(2,1)S(1)} %collective-permute-done.2.sibling.rest_0_, ...), custom_call_target="tpu_custom_call" | custom-call | flops 1000000000 | bytes 1048576 | tf_op jit(solution)/shard_map/pallas_call | solution.py:480
  51.2 0.0 collective-permute-done.left
  51.2 0.0 collective-permute-done.1.right
  51.2 19.1 %shard_map.98 = f32[32,4096]{1,0:T(8,128)} custom-call(s32[2,512]{1,0:T(2,128)S(1)} %copy-done.4, bf16[96,4096]{1,0:T(8,128)(2,1)S(1)} %collective-permute-done.left, bf16[96,4096]{1,0:T(8,128)(2,1)S(1)} %collective-permute-done.1.right, bf16[30,128,256]{2,1,0:T(8,128)(2,1)S(1)} %get-tuple-element.26.src.own_src, ...), custom_call_target="tpu_custom_call" | custom-call | flops 10000000000 | bytes 1048576 | tf_op jit(solution)/shard_map/pallas_call | solution.py:488
  (5 shorter events, 0.0 us)
Async XLA Ops:
  0.6 14.3 %copy-start.2 = (s32[15,256]{1,0:T(8,128)S(1)}, s32[15,256]{1,0:T(8,128)}, u32[]{:S(2)}) copy-start(s32[15,256]{1,0:T(8,128)} %skel.5) | copy-start | bytes 46084
  7.6 43.6 %collective-permute-start = (bf16[96,4096]{1,0:T(8,128)(2,1)}, bf16[96,4096]{1,0:T(8,128)(2,1)S(1)}, u32[]{:S(2)}, u32[]{:S(2)}) collective-permute-start(bf16[96,4096]{1,0:T(8,128)(2,1)} %get-tuple-element.25.stacked), channel_id=1, source_target_pairs={{0,1},{1,2},{2,3},{3,4},{4,5},{5,6},{6,7},{7,8},{8,9},{9,10},{10,1... | collective-permute-start | bytes 2359304 | tf_op jit(solution)/shard_map/ppermute | solution.py:431
  9.5 41.7 %collective-permute-start.1 = (bf16[96,4096]{1,0:T(8,128)(2,1)}, bf16[96,4096]{1,0:T(8,128)(2,1)S(1)}, u32[]{:S(2)}, u32[]{:S(2)}) collective-permute-start(bf16[96,4096]{1,0:T(8,128)(2,1)} %get-tuple-element.25.stacked), channel_id=1, source_target_pairs={{1,0},{2,1},{3,2},{4,3},{5,4},{6,5},{7,6},{8,7},{9,8},{10,9},{11,1... | collective-permute-start | bytes 2359304 | tf_op jit(solution)/shard_map/ppermute | solution.py:432
  14.9 1.1 %copy-start.1 = (bf16[96,4096]{1,0:T(8,128)(2,1)S(1)}, bf16[96,4096]{1,0:T(8,128)(2,1)}, u32[]{:S(2)}) copy-start(bf16[96,4096]{1,0:T(8,128)(2,1)} %get-tuple-element.25.stacked) | copy-start | bytes 2359300
  16.1 6.0 %copy-start.4 = (s32[2,512]{1,0:T(2,128)S(1)}, s32[2,512]{1,0:T(2,128)}, u32[]{:S(2)}) copy-start(s32[2,512]{1,0:T(2,128)} %get-tuple-element.24.pairs) | copy-start | bytes 12292
  22.0 3.4 %collective-permute-start.2 = (bf16[112,256]{1,0:T(8,128)(2,1)S(1)}, bf16[112,256]{1,0:T(8,128)(2,1)S(1)}, u32[]{:S(2)}, u32[]{:S(2)}) collective-permute-start(bf16[112,256]{1,0:T(8,128)(2,1)S(1)} %get-tuple-element.30._.own), channel_id=1, source_target_pairs={{0,1},{1,0},{2,3},{3,2},{4,5},{5,4},{6,7},{7,6},{8,9},{9,8},{10,11... | collective-permute-start | bytes 172040 | tf_op jit(solution)/shard_map/ppermute | solution.py:453
  22.1 3.3 %copy-start = (s32[30,256]{1,0:T(8,128)S(1)}, s32[30,256]{1,0:T(8,128)}, u32[]{:S(2)}) copy-start(s32[30,256]{1,0:T(8,128)} %skel.9) | copy-start | bytes 92164
  26.1 5.5 %collective-permute-start.3 = (bf16[112,256]{1,0:T(8,128)(2,1)S(1)}, bf16[112,256]{1,0:T(8,128)(2,1)S(1)}, u32[]{:S(2)}, u32[]{:S(2)}) collective-permute-start(bf16[112,256]{1,0:T(8,128)(2,1)S(1)} %get-tuple-element.31._.own), channel_id=1, source_target_pairs={{0,2},{1,3},{2,0},{3,1},{4,6},{5,7},{6,4},{7,5},{8,10},{9,11},{10,... | collective-permute-start | bytes 172040 | tf_op jit(solution)/shard_map/ppermute | solution.py:453
  32.4 4.9 %collective-permute-start.4 = (bf16[112,256]{1,0:T(8,128)(2,1)S(1)}, bf16[112,256]{1,0:T(8,128)(2,1)S(1)}, u32[]{:S(2)}, u32[]{:S(2)}) collective-permute-start(bf16[112,256]{1,0:T(8,128)(2,1)S(1)} %get-tuple-element.32._.own), channel_id=1, source_target_pairs={{0,4},{1,5},{2,6},{3,7},{4,0},{5,1},{6,2},{7,3},{8,12},{9,13},{10,... | collective-permute-start | bytes 172040 | tf_op jit(solution)/shard_map/ppermute | solution.py:453
  38.0 4.2 %collective-permute-start.5 = (bf16[112,256]{1,0:T(8,128)(2,1)S(1)}, bf16[112,256]{1,0:T(8,128)(2,1)S(1)}, u32[]{:S(2)}, u32[]{:S(2)}) collective-permute-start(bf16[112,256]{1,0:T(8,128)(2,1)S(1)} %get-tuple-element.33._.own), channel_id=1, source_target_pairs={{0,8},{1,9},{2,10},{3,11},{4,12},{5,13},{6,14},{7,15},{8,0},{9,1},... | collective-permute-start | bytes 172040 | tf_op jit(solution)/shard_map/ppermute | solution.py:453
  43.0 5.9 %collective-permute-start.6 = (bf16[112,256]{1,0:T(8,128)(2,1)S(1)}, bf16[112,256]{1,0:T(8,128)(2,1)S(1)}, u32[]{:S(2)}, u32[]{:S(2)}) collective-permute-start(bf16[112,256]{1,0:T(8,128)(2,1)S(1)} %get-tuple-element.34._), channel_id=1, source_target_pairs={{0,16},{1,17},{2,18},{3,19},{4,20},{5,21},{6,22},{7,23},{8,24},{9,... | collective-permute-start | bytes 172040 | tf_op jit(solution)/shard_map/ppermute | solution.py:453
  48.9 2.3 %copy-start.3 = (s32[1,4096]{1,0:T(1,128)S(1)}, s32[1,4096]{1,0:T(1,128)}, u32[]{:S(2)}) copy-start(s32[1,4096]{1,0:T(1,128)} %order.3) | copy-start | bytes 49156

commit v2 on v1

--- a/solution.py
+++ b/solution.py
@@ -16,8 +16,8 @@
 AUX = 8
 DEPTH = 128
 BATCH, SMALL = 24, 8
-FILL = 28
-FILLERS = 5
+OWN_PARTS = (72, 72)
+ANY_PARTS = (28, 36, 36)
 UNROLL = 4
 VMEM = pl.BlockSpec(memory_space=pltpu.VMEM)
 SMEM = pl.BlockSpec(memory_space=pltpu.SMEM)
@@ -303,12 +303,44 @@
     lax.fori_loop(0, (total - large * BATCH + (SMALL - 1)) // SMALL, small_step, 0)
 
 
-def own_kernel(kern_scale, part, pairs, src, tgt, wts, _, *rest):
+def fixed_pairs(kern_scale, start, count, pairs, src, tgt, wts, acc, first=0):
+    def step(i, carry):
+        codes = [pairs[0, start + i * size + u] for u in range(size)]
+        pair_terms(kern_scale, codes, src, tgt, wts, acc, first)
+        return carry
+
+    size = count if count <= 36 else BATCH
+    lax.fori_loop(0, count // size, step, 0)
+
+
+def own_kernel(kern_scale, start, count, pairs, src, tgt, wts, _, *rest):
     acc = rest[-1]
-    if part == 0:
+    if start == 0:
         acc[...] = jnp.zeros_like(acc)
-    codes = [pairs[0, part * FILL + u] for u in range(FILL)]
-    pair_terms(kern_scale, codes, src, tgt, wts, acc, (src.shape[0] + 2) // 2)
+    fixed_pairs(kern_scale, start, count, pairs, src, tgt, wts, acc, (src.shape[0] + 2) // 2)
+
+
+def meet_kernel(
+    kern_scale, features, start, count, pairs, place, within, across, own_src, tgt, own_wts, _, _acc,
+    acc, src, wts,
+):
+    leaves = src.shape[0] // 3
+    width = src.shape[2]
+    odd = place[0] & 1
+    for halo, side in ((within, 2 - 2 * odd), (across, 2 * odd)):
+        for leaf in range(leaves):
+            cols = pl.ds(leaf * width, width)
+            x = halo[:features, cols].astype(F32)
+            at = side * leaves + leaf
+            src[at] = source_form(x, *aux_rows(x))
+            wts[at] = halo[features:, cols]
+    src[pl.ds(leaves, leaves)] = own_src[pl.ds(0, leaves)]
+    wts[pl.ds(leaves, leaves)] = own_wts[pl.ds(0, leaves)]
+    fixed_pairs(kern_scale, start, count, pairs, src, tgt, wts, acc)
+
+
+def any_kernel(kern_scale, start, count, pairs, src, tgt, wts, _, _acc, acc):
+    fixed_pairs(kern_scale, start, count, pairs, src, tgt, wts, acc)
 
 
 def down_kernel(kern_scale, upper, live, kernels, acc, *rest):
@@ -346,27 +378,18 @@
 
 
 def final_kernel(
-    kern_scale, features, fixed, pairs, left, right, own_src, own_wts, tgt, order, leaf_field, own_acc,
-    out, src, wts, acc, spread,
+    kern_scale, fixed, pairs, src, tgt, wts, order, leaf_field, all_acc, out, acc, spread
 ):
     leaves = leaf_field.shape[0]
     width = leaf_field.shape[2]
     rhs = out.shape[0]
-    for side, halo in ((0, left), (2, right)):
-        for leaf in range(leaves):
-            cols = pl.ds(leaf * width, width)
-            x = halo[:features, cols].astype(F32)
-            src[side * leaves + leaf] = source_form(x, *aux_rows(x))
-            wts[side * leaves + leaf] = halo[features:, cols]
-    src[pl.ds(leaves, leaves)] = own_src[pl.ds(0, leaves)]
-    wts[pl.ds(leaves, leaves)] = own_wts[pl.ds(0, leaves)]
-    acc[...] = own_acc[pl.ds(0, leaves)] + leaf_field[...]
+    acc[...] = all_acc[pl.ds(0, leaves)] + leaf_field[...]
 
     def batch(first, size):
         codes = [pairs[0, fixed + first + u] for u in range(size)]
         pair_terms(kern_scale, codes, src, tgt, wts, acc)
 
-    pair_loop(pairs[1, 0] - fixed, batch)
+    pair_loop(jnp.maximum(pairs[1, 0] - fixed, 0), batch)
     spread[...] = jnp.zeros_like(spread)
     span = UNROLL * width
 
@@ -408,10 +431,9 @@
     place = jnp.reshape(position, (1,)).astype(jnp.int32)
 
     half = leaves // 2
-    fillers = min(FILLERS, upper)
-    fixed = fillers * FILL
-    pairs_most = near_list.size + half * half + half - 2
-    length = -(-(max(pairs_most, near_list.size + fixed) + BATCH) // 128) * 128
+    fixed = sum(OWN_PARTS)
+    most = near_list.size + max(half * half + half - 2, fixed)
+    length = -(-(max(most, fixed + sum(ANY_PARTS)) + BATCH) // 128) * 128
     stacked, pairs = call(
         functools.partial(gather_kernel, fixed),
         (shape((rows, total), BF), shape((2, length), jnp.int32)),
@@ -427,10 +449,10 @@
         10**10,
         limit_mb=63,
     )(points, charges, leaf_order, near_list, far_list, place)
-    ring = list(range(devices - 1))
-    left = lax.ppermute(stacked, "leaf", [(i, i + 1) for i in ring])
-    right = lax.ppermute(stacked, "leaf", [(i + 1, i) for i in ring])
-
+    within = lax.ppermute(stacked, "leaf", [(i, i ^ 1) for i in range(devices)])
+    across = lax.ppermute(
+        stacked, "leaf", [(i, i + 1 if i % 2 else i - 1) for i in range(1, devices - 1)]
+    )
     known = leaves + nodes - 1
     srcs, tgts, wtss, kernels, own, own_tgt = call(
         functools.partial(tree_kernel, kern_scale, features),
@@ -447,19 +469,58 @@
         10**10,
     )(stacked, local_skel)
 
+    def own_part(start, count, after, acc):
+        return call(
+            functools.partial(own_kernel, kern_scale, start, count),
+            shape((known, rhs, width), F32),
+            [SMEM] + [VMEM] * 3 + [ANY] + [VMEM] * (start > 0),
+            [],
+            10**10,
+            aliases={5: 0} if start else None,
+        )(pairs, srcs, tgts, wtss, after, *([acc] if start else []))
+
+    def meet_part(start, count, after, acc):
+        return call(
+            functools.partial(meet_kernel, kern_scale, features, start, count),
+            (
+                shape((known, rhs, width), F32),
+                shape((3 * leaves, DEPTH, width), BF),
+                shape((3 * leaves, rhs, width), BF),
+            ),
+            [SMEM] * 2 + [VMEM] * 5 + [ANY, VMEM],
+            [],
+            10**10,
+            aliases={8: 0},
+        )(pairs, place, within, across, srcs, tgts, wtss, after, acc)
+
+    def any_part(start, count, after, acc):
+        return call(
+            functools.partial(any_kernel, kern_scale, start, count),
+            shape((known, rhs, width), F32),
+            [SMEM] + [VMEM] * 3 + [ANY, VMEM],
+            [],
+            10**10,
+            aliases={5: 0},
+        )(pairs, all_src, tgts, all_wts, after, acc)
+
     siblings, targets, half_kernels = [], [], []
-    acc = None
+    acc = all_src = all_wts = None
+    taken = 0
     for bit in range(upper):
         sibling = lax.ppermute(own, "leaf", [(i, i ^ (1 << bit)) for i in range(devices)])
-        if bit < fillers:
-            acc = call(
-                functools.partial(own_kernel, kern_scale, bit),
-                shape((known, rhs, width), F32),
-                [SMEM] + [VMEM] * 3 + [ANY] + [VMEM] * (bit > 0),
-                [],
-                4 * 10**9,
-                aliases={5: 0} if bit else None,
-            )(pairs, srcs, tgts, wtss, own, *([acc] if bit else []))
+        part = bit - len(OWN_PARTS)
+        if part < 0:
+            count = OWN_PARTS[bit]
+            acc = own_part(taken, count, own, acc)
+        elif part < len(ANY_PARTS):
+            count = ANY_PARTS[part]
+            if part == 0:
+                acc, all_src, all_wts = meet_part(taken, count, own, acc)
+            else:
+                acc = any_part(taken, count, own, acc)
+        else:
+            count = 0
+        taken += count
         siblings.append(sibling)
         targets.append(own_tgt)
         if bit == upper - 1:
@@ -486,17 +547,12 @@
     )(kernels, acc, *siblings, *targets, *half_kernels)
 
     potentials = call(
-        functools.partial(final_kernel, kern_scale, features, fixed),
+        functools.partial(final_kernel, kern_scale, taken),
         shape((rhs, total), F32),
-        [SMEM] + [VMEM] * 8,
-        [
-            pltpu.VMEM((3 * leaves, DEPTH, width), BF),
-            pltpu.VMEM((3 * leaves, rhs, width), BF),
-            pltpu.VMEM((leaves, rhs, width), F32),
-            pltpu.VMEM((leaves * 2 * rhs, width), F32),
-        ],
+        [SMEM] + [VMEM] * 6,
+        [pltpu.VMEM((leaves, rhs, width), F32), pltpu.VMEM((leaves * 2 * rhs, width), F32)],
         10**10,
-    )(pairs, left, right, srcs, wtss, tgts, leaf_order, leaf_field, acc)
+    )(pairs, all_src, tgts, all_wts, leaf_order, leaf_field, acc)
     return (potentials, root[None])
 
 

time: 70.4 us -> 65.9 us (0.936)
  waiting for transfers between devices: 3.16 us -> 0.02 us
  starting transfers between devices: 11.7 us -> 9.97 us
    ppermute x2, starting transfers between devices: 7.36 us -> 3.75 us  [the longest x1 3.68 us: local(): lax.ppermute(stacked, 'leaf', [(i, i + 1 if i % 2 else i - 1) for i in ra...]
    ppermute x5, waiting for transfers between devices: 3.15 us -> 0.02 us  [local(): lax.ppermute(own, 'leaf', [(i, i ^ 1 << bit) for i in range(devices)])]
    ppermute x5, starting transfers between devices: 4.33 us -> 6.22 us  [local(): lax.ppermute(own, 'leaf', [(i, i ^ 1 << bit) for i in range(devices)])]
  transfers between devices with their start and end apart: 7 -> 7, of which waited for: 2 -> 0; matrix products, arithmetic and copies ran while one was open for 0% -> 0% of each run, Pallas kernels for 39% -> 52%
where the time goes in v2:
time: 65.9 us; the launch traced here: 65.6 us
  Pallas kernels  53.6 us (81%)
  starting transfers between devices  9.97 us (15%)
  local copies, waits for them, and re-layouts  1.14 us (2%)
  between operations  0.82 us (1%)
    pallas_call x2, Pallas kernels, own_part(): call(functools.partial(own_kernel, kern_scale, start, count), shape((know...  15.3 us
    pallas_call x1, Pallas kernels, local(): call(functools.partial(final_kernel, kern_scale, taken), shape((rhs, tota...  8.71 us
    pallas_call x2, Pallas kernels, any_part(): call(functools.partial(any_kernel, kern_scale, start, count), shape((know...  7.85 us
    pallas_call x1, Pallas kernels, local(): call(functools.partial(gather_kernel, fixed), (shape((rows, total), BF),...  6.9 us
    ppermute x5, starting transfers between devices, local(): lax.ppermute(own, 'leaf', [(i, i ^ 1 << bit) for i in range(devices)])  6.22 us
    pallas_call x1, Pallas kernels, local(): call(functools.partial(tree_kernel, kern_scale, features), (shape((known,...  5.92 us
    ppermute x1, starting transfers between devices, local(): lax.ppermute(stacked, 'leaf', [(i, i + 1 if i % 2 else i - 1) for i in ra...  3.68 us
    pallas_call x1, Pallas kernels, meet_part(): call(functools.partial(meet_kernel, kern_scale, features, start, count),...  3.62 us
  transfers between devices with their start and end apart: 7, of which 0 were waited for; matrix products, arithmetic and copies ran while one was open for 0% of the time, Pallas kernels for 52%

profile of v2, /device:TPU:8, one launch (start us, length us, event | category | flops | bytes accessed | tf_op | source)
XLA Modules:
  0.0 65.6 jit_solution(16964427228394501463)
XLA Ops:
  0.6 0.0 copy-start.2
  0.6 6.9 %shard_map.86 = (bf16[96,4096]{1,0:T(8,128)(2,1)}, s32[2,512]{1,0:T(2,128)}) custom-call(bf16[64,4096]{1,0:T(8,128)(2,1)} %points.1, bf16[32,4096]{1,0:T(8,128)(2,1)} %charges.1, s32[1,4096]{1,0:T(1,128)} %order.3, s32[16,16]{1,0:T(8,128)} %near.1, s32[8,8]{1,0:T(8,128)} %far.1, s32[1]{0:T(128)} %bitcast.place), custom_call_target="tpu_custom_call" | custom-call | flops 10000000000 | bytes 1048576 | tf_op jit(solution)/shard_map/pallas_call | solution.py:437
  7.5 3.7 %collective-permute-start.1 = (bf16[96,4096]{1,0:T(8,128)(2,1)}, bf16[96,4096]{1,0:T(8,128)(2,1)S(1)}, u32[]{:S(2)}, u32[]{:S(2)}) collective-permute-start(bf16[96,4096]{1,0:T(8,128)(2,1)} %get-tuple-element.28.stacked), channel_id=1, source_target_pairs={{1,2},{2,1},{3,4},{4,3},{5,6},{6,5},{7,8},{8,7},{9,10},{10,9},{11,... | collective-permute-start | bytes 2359304 | tf_op jit(solution)/shard_map/ppermute | solution.py:453
  11.2 0.1 collective-permute-start
  11.3 0.0 copy-done.2
  11.3 1.1 %copy-done.1 = bf16[96,4096]{1,0:T(8,128)(2,1)S(1)} copy-done((bf16[96,4096]{1,0:T(8,128)(2,1)S(1)}, bf16[96,4096]{1,0:T(8,128)(2,1)}, u32[]{:S(2)}) %copy-start.1) | copy-done | bytes 786456
  12.5 5.9 %shard_map.87 = (bf16[30,128,256]{2,1,0:T(8,128)(2,1)S(1)}, bf16[30,256,128]{2,1,0:T(8,128)(2,1)S(1)}, bf16[30,32,256]{2,1,0:T(8,128)(2,1)S(1)}, bf16[15,256,512...) custom-call(bf16[96,4096]{1,0:T(8,128)(2,1)S(1)} %copy-done.1, s32[15,256]{1,0:T(8,128)S(1)} %copy-done.2), custom_call_target="tpu_custom_call" | custom-call | flops 10000000000 | bytes 1048576 | tf_op jit(solution)/shard_map/pallas_call | solution.py:457
  18.4 0.6 collective-permute-start.2
  18.9 7.6 %shard_map.88._.rest_0_ = f32[30,32,256]{2,1,0:T(8,128)S(1)} custom-call(s32[2,512]{1,0:T(2,128)S(1)} %copy-done.4, bf16[30,128,256]{2,1,0:T(8,128)(2,1)S(1)} %get-tuple-element.29.src.own_src, bf16[30,256,128]{2,1,0:T(8,128)(2,1)S(1)} %get-tuple-element.30.tgt, bf16[30,32,256]{2,1,0:T(8,128)(2,1)S(1)} %get-tuple-element.31.wts.own_wts, ...), custom_call_target="tpu_custom_call" | custom-call | flops 10000000000 | bytes 1048576 | tf_op jit(solution)/shard_map/pallas_call | solution.py:473
  26.6 0.0 collective-permute-done.2.sibling.rest_0_
  26.6 0.7 %shard_map.89 = (bf16[112,256]{1,0:T(8,128)(2,1)S(1)}, bf16[256,128]{1,0:T(8,128)(2,1)S(1)}, bf16[256,256]{1,0:T(8,128)(2,1)S(1)}) custom-call(s32[1]{0:T(128)} %bitcast.place, bf16[112,256]{1,0:T(8,128)(2,1)S(1)} %get-tuple-element.32._.own, bf16[112,256]{1,0:T(8,128)(2,1)S(1)} %collective-permute-done.2.sibling.rest_0_, s32[30,256]{1,0:T(8,128)S(1)} %copy-done, ...), custom_call_target="tpu_custom_call" | custom-call | flops 100000000 | bytes 1048576 | tf_op jit(solution)/shard_map/pallas_call | solution.py:528
  27.3 0.9 %collective-permute-start.3 = (bf16[112,256]{1,0:T(8,128)(2,1)S(1)}, bf16[112,256]{1,0:T(8,128)(2,1)S(1)}, u32[]{:S(2)}, u32[]{:S(2)}) collective-permute-start(bf16[112,256]{1,0:T(8,128)(2,1)S(1)} %get-tuple-element.33._.own), channel_id=1, source_target_pairs={{0,2},{1,3},{2,0},{3,1},{4,6},{5,7},{6,4},{7,5},{8,10},{9,11},{10,... | collective-permute-start | bytes 172040 | tf_op jit(solution)/shard_map/ppermute | solution.py:510
  28.2 7.7 %shard_map.90._._acc = f32[30,32,256]{2,1,0:T(8,128)S(1)} custom-call(s32[2,512]{1,0:T(2,128)S(1)} %copy-done.4, bf16[30,128,256]{2,1,0:T(8,128)(2,1)S(1)} %get-tuple-element.29.src.own_src, bf16[30,256,128]{2,1,0:T(8,128)(2,1)S(1)} %get-tuple-element.30.tgt, bf16[30,32,256]{2,1,0:T(8,128)(2,1)S(1)} %get-tuple-element.31.wts.own_wts, ...), custom_call_target="tpu_custom_call", output_to_operand_aliasing={{}: (5, {})} | custom-call | flops 10000000000 | bytes 1048576 | tf_op jit(solution)/shard_map/pallas_call | solution.py:473
  35.9 0.0 collective-permute-done.3.sibling.rest_1_
  35.9 0.7 %shard_map.91 = (bf16[112,256]{1,0:T(8,128)(2,1)S(1)}, bf16[256,128]{1,0:T(8,128)(2,1)S(1)}, bf16[256,256]{1,0:T(8,128)(2,1)S(1)}) custom-call(s32[1]{0:T(128)} %bitcast.place, bf16[112,256]{1,0:T(8,128)(2,1)S(1)} %get-tuple-element.33._.own, bf16[112,256]{1,0:T(8,128)(2,1)S(1)} %collective-permute-done.3.sibling.rest_1_, s32[30,256]{1,0:T(8,128)S(1)} %copy-done, ...), custom_call_target="tpu_custom_call" | custom-call | flops 100000000 | bytes 1048576 | tf_op jit(solution)/shard_map/pallas_call | solution.py:528
  36.6 1.6 %collective-permute-start.4 = (bf16[112,256]{1,0:T(8,128)(2,1)S(1)}, bf16[112,256]{1,0:T(8,128)(2,1)S(1)}, u32[]{:S(2)}, u32[]{:S(2)}) collective-permute-start(bf16[112,256]{1,0:T(8,128)(2,1)S(1)} %get-tuple-element.34._.own), channel_id=1, source_target_pairs={{0,4},{1,5},{2,6},{3,7},{4,0},{5,1},{6,2},{7,3},{8,12},{9,13},{10,... | collective-permute-start | bytes 172040 | tf_op jit(solution)/shard_map/ppermute | solution.py:510
  38.2 0.0 collective-permute-done.1.across
  38.2 0.0 collective-permute-done.within
  38.2 3.6 %shard_map.92 = (f32[30,32,256]{2,1,0:T(8,128)S(1)}, bf16[48,128,256]{2,1,0:T(8,128)(2,1)S(1)}, bf16[48,32,256]{2,1,0:T(8,128)(2,1)S(1)}) custom-call(s32[2,512]{1,0:T(2,128)S(1)} %copy-done.4, s32[1]{0:T(128)} %bitcast.place, bf16[96,4096]{1,0:T(8,128)(2,1)S(1)} %collective-permute-done.within, ...), custom_call_target="tpu_custom_call", output_to_operand_aliasing={{0}: (8, {})} | custom-call | flops 10000000000 | bytes 1048576 | tf_op jit(solution)/shard_map/pallas_call | solution.py:483
  41.8 0.0 collective-permute-done.4.sibling.rest_2_
  41.8 0.7 %shard_map.93 = (bf16[112,256]{1,0:T(8,128)(2,1)S(1)}, bf16[256,128]{1,0:T(8,128)(2,1)S(1)}, bf16[256,256]{1,0:T(8,128)(2,1)S(1)}) custom-call(s32[1]{0:T(128)} %bitcast.place, bf16[112,256]{1,0:T(8,128)(2,1)S(1)} %get-tuple-element.34._.own, bf16[112,256]{1,0:T(8,128)(2,1)S(1)} %collective-permute-done.4.sibling.rest_2_, s32[30,256]{1,0:T(8,128)S(1)} %copy-done, ...), custom_call_target="tpu_custom_call" | custom-call | flops 100000000 | bytes 1048576 | tf_op jit(solution)/shard_map/pallas_call | solution.py:528
  42.5 0.5 collective-permute-start.5
  43.1 3.9 %shard_map.94._._acc = f32[30,32,256]{2,1,0:T(8,128)S(1)} custom-call(s32[2,512]{1,0:T(2,128)S(1)} %copy-done.4, bf16[48,128,256]{2,1,0:T(8,128)(2,1)S(1)} %get-tuple-element.35.src, bf16[30,256,128]{2,1,0:T(8,128)(2,1)S(1)} %get-tuple-element.30.tgt, bf16[48,32,256]{2,1,0:T(8,128)(2,1)S(1)} %get-tuple-element.36.wts, ...), custom_call_target="tpu_custom_call", output_to_operand_aliasing={{}: (5, {})} | custom-call | flops 10000000000 | bytes 1048576 | tf_op jit(solution)/shard_map/pallas_call | solution.py:497
  47.0 0.0 collective-permute-done.5.sibling.rest_3_
  47.0 0.7 %shard_map.95 = (bf16[112,256]{1,0:T(8,128)(2,1)S(1)}, bf16[256,128]{1,0:T(8,128)(2,1)S(1)}, bf16[256,256]{1,0:T(8,128)(2,1)S(1)}) custom-call(s32[1]{0:T(128)} %bitcast.place, bf16[112,256]{1,0:T(8,128)(2,1)S(1)} %get-tuple-element.39._.own, bf16[112,256]{1,0:T(8,128)(2,1)S(1)} %collective-permute-done.5.sibling.rest_3_, s32[30,256]{1,0:T(8,128)S(1)} %copy-done, ...), custom_call_target="tpu_custom_call" | custom-call | flops 100000000 | bytes 1048576 | tf_op jit(solution)/shard_map/pallas_call | solution.py:528
  47.7 2.6 %collective-permute-start.6 = (bf16[112,256]{1,0:T(8,128)(2,1)S(1)}, bf16[112,256]{1,0:T(8,128)(2,1)S(1)}, u32[]{:S(2)}, u32[]{:S(2)}) collective-permute-start(bf16[112,256]{1,0:T(8,128)(2,1)S(1)} %get-tuple-element.40._), channel_id=1, source_target_pairs={{0,16},{1,17},{2,18},{3,19},{4,20},{5,21},{6,22},{7,23},{8,24},{9,... | collective-permute-start | bytes 172040 | tf_op jit(solution)/shard_map/ppermute | solution.py:510
  50.4 3.9 %shard_map.96.acc.all_acc = f32[30,32,256]{2,1,0:T(8,128)S(1)} custom-call(s32[2,512]{1,0:T(2,128)S(1)} %copy-done.4, bf16[48,128,256]{2,1,0:T(8,128)(2,1)S(1)} %get-tuple-element.35.src, bf16[30,256,128]{2,1,0:T(8,128)(2,1)S(1)} %get-tuple-element.30.tgt, bf16[48,32,256]{2,1,0:T(8,128)(2,1)S(1)} %get-tuple-element.36.wts, ...), custom_call_target="tpu_custom_call", output_to_operand_aliasing={{}: (5, {})} | custom-call | flops 10000000000 | bytes 1048576 | tf_op jit(solution)/shard_map/pallas_call | solution.py:497
  54.3 0.0 copy-start.3
  54.3 0.0 collective-permute-done.6.rest_4_
  54.3 2.5 %shard_map.97 = (f32[32,256]{1,0:T(8,128)}, f32[16,32,256]{2,1,0:T(8,128)S(1)}) custom-call(bf16[15,256,512]{2,1,0:T(8,128)(2,1)S(1)} %get-tuple-element.37.kernels, f32[30,32,256]{2,1,0:T(8,128)S(1)} %shard_map.96.acc.all_acc, bf16[112,256]{1,0:T(8,128)(2,1)S(1)} %collective-permute-done.2.sibling.rest_0_, ...), custom_call_target="tpu_custom_call" | custom-call | flops 1000000000 | bytes 1048576 | tf_op jit(solution)/shard_map/pallas_call | solution.py:541
  56.8 0.0 copy-done.3
  56.8 8.7 %shard_map.98 = f32[32,4096]{1,0:T(8,128)} custom-call(s32[2,512]{1,0:T(2,128)S(1)} %copy-done.4, bf16[48,128,256]{2,1,0:T(8,128)(2,1)S(1)} %get-tuple-element.35.src, bf16[30,256,128]{2,1,0:T(8,128)(2,1)S(1)} %get-tuple-element.30.tgt, bf16[48,32,256]{2,1,0:T(8,128)(2,1)S(1)} %get-tuple-element.36.wts, s32[1,4096]{1,0:T(1,128)S(1)} %copy-done.3, ...), custom_call_target="tpu_custom_call" | custom-call | flops 10000000000 | bytes 1048576 | tf_op jit(solution)/shard_map/pallas_call | solution.py:549
  (5 shorter events, 0.0 us)
Async XLA Ops:
  0.6 10.7 %copy-start.2 = (s32[15,256]{1,0:T(8,128)S(1)}, s32[15,256]{1,0:T(8,128)}, u32[]{:S(2)}) copy-start(s32[15,256]{1,0:T(8,128)} %skel.5) | copy-start | bytes 46084
  7.5 30.6 %collective-permute-start.1 = (bf16[96,4096]{1,0:T(8,128)(2,1)}, bf16[96,4096]{1,0:T(8,128)(2,1)S(1)}, u32[]{:S(2)}, u32[]{:S(2)}) collective-permute-start(bf16[96,4096]{1,0:T(8,128)(2,1)} %get-tuple-element.28.stacked), channel_id=1, source_target_pairs={{1,2},{2,1},{3,4},{4,3},{5,6},{6,5},{7,8},{8,7},{9,10},{10,9},{11,... | collective-permute-start | bytes 2359304 | tf_op jit(solution)/shard_map/ppermute | solution.py:453
  11.2 26.9 %collective-permute-start = (bf16[96,4096]{1,0:T(8,128)(2,1)}, bf16[96,4096]{1,0:T(8,128)(2,1)S(1)}, u32[]{:S(2)}, u32[]{:S(2)}) collective-permute-start(bf16[96,4096]{1,0:T(8,128)(2,1)} %get-tuple-element.28.stacked), channel_id=1, source_target_pairs={{0,1},{1,0},{2,3},{3,2},{4,5},{5,4},{6,7},{7,6},{8,9},{9,8},{10,11... | collective-permute-start | bytes 2359304 | tf_op jit(solution)/shard_map/ppermute | solution.py:452
  11.3 1.1 %copy-start.1 = (bf16[96,4096]{1,0:T(8,128)(2,1)S(1)}, bf16[96,4096]{1,0:T(8,128)(2,1)}, u32[]{:S(2)}) copy-start(bf16[96,4096]{1,0:T(8,128)(2,1)} %get-tuple-element.28.stacked) | copy-start | bytes 2359300
  12.5 6.5 %copy-start.4 = (s32[2,512]{1,0:T(2,128)S(1)}, s32[2,512]{1,0:T(2,128)}, u32[]{:S(2)}) copy-start(s32[2,512]{1,0:T(2,128)} %get-tuple-element.27.pairs) | copy-start | bytes 12292
  18.4 8.2 %collective-permute-start.2 = (bf16[112,256]{1,0:T(8,128)(2,1)S(1)}, bf16[112,256]{1,0:T(8,128)(2,1)S(1)}, u32[]{:S(2)}, u32[]{:S(2)}) collective-permute-start(bf16[112,256]{1,0:T(8,128)(2,1)S(1)} %get-tuple-element.32._.own), channel_id=1, source_target_pairs={{0,1},{1,0},{2,3},{3,2},{4,5},{5,4},{6,7},{7,6},{8,9},{9,8},{10,11... | collective-permute-start | bytes 172040 | tf_op jit(solution)/shard_map/ppermute | solution.py:510
  18.9 7.6 %copy-start = (s32[30,256]{1,0:T(8,128)S(1)}, s32[30,256]{1,0:T(8,128)}, u32[]{:S(2)}) copy-start(s32[30,256]{1,0:T(8,128)} %skel.9) | copy-start | bytes 92164
  27.3 8.6 %collective-permute-start.3 = (bf16[112,256]{1,0:T(8,128)(2,1)S(1)}, bf16[112,256]{1,0:T(8,128)(2,1)S(1)}, u32[]{:S(2)}, u32[]{:S(2)}) collective-permute-start(bf16[112,256]{1,0:T(8,128)(2,1)S(1)} %get-tuple-element.33._.own), channel_id=1, source_target_pairs={{0,2},{1,3},{2,0},{3,1},{4,6},{5,7},{6,4},{7,5},{8,10},{9,11},{10,... | collective-permute-start | bytes 172040 | tf_op jit(solution)/shard_map/ppermute | solution.py:510
  36.6 5.2 %collective-permute-start.4 = (bf16[112,256]{1,0:T(8,128)(2,1)S(1)}, bf16[112,256]{1,0:T(8,128)(2,1)S(1)}, u32[]{:S(2)}, u32[]{:S(2)}) collective-permute-start(bf16[112,256]{1,0:T(8,128)(2,1)S(1)} %get-tuple-element.34._.own), channel_id=1, source_target_pairs={{0,4},{1,5},{2,6},{3,7},{4,0},{5,1},{6,2},{7,3},{8,12},{9,13},{10,... | collective-permute-start | bytes 172040 | tf_op jit(solution)/shard_map/ppermute | solution.py:510
  42.5 4.5 %collective-permute-start.5 = (bf16[112,256]{1,0:T(8,128)(2,1)S(1)}, bf16[112,256]{1,0:T(8,128)(2,1)S(1)}, u32[]{:S(2)}, u32[]{:S(2)}) collective-permute-start(bf16[112,256]{1,0:T(8,128)(2,1)S(1)} %get-tuple-element.39._.own), channel_id=1, source_target_pairs={{0,8},{1,9},{2,10},{3,11},{4,12},{5,13},{6,14},{7,15},{8,0},{9,1},... | collective-permute-start | bytes 172040 | tf_op jit(solution)/shard_map/ppermute | solution.py:510
  47.7 6.6 %collective-permute-start.6 = (bf16[112,256]{1,0:T(8,128)(2,1)S(1)}, bf16[112,256]{1,0:T(8,128)(2,1)S(1)}, u32[]{:S(2)}, u32[]{:S(2)}) collective-permute-start(bf16[112,256]{1,0:T(8,128)(2,1)S(1)} %get-tuple-element.40._), channel_id=1, source_target_pairs={{0,16},{1,17},{2,18},{3,19},{4,20},{5,21},{6,22},{7,23},{8,24},{9,... | collective-permute-start | bytes 172040 | tf_op jit(solution)/shard_map/ppermute | solution.py:510
  54.3 2.5 %copy-start.3 = (s32[1,4096]{1,0:T(1,128)S(1)}, s32[1,4096]{1,0:T(1,128)}, u32[]{:S(2)}) copy-start(s32[1,4096]{1,0:T(1,128)} %order.3) | copy-start | bytes 49156
